TPU v7x, 32 devices: a whole 2x2x4 slice. The times are simulated.
32 devices in a mesh: dp: 4 (over z), vocab: 8 (over y, x, core).
Axes of the slice: x: 2, y: 2, z: 4, core: 2. Of those that a mesh axis runs over, the one named last changes fastest.
Arguments:
- hidden: bfloat16 [4, 2, 64, 4608], P('dp'), may hold values from -6 to 6
- table: bfloat16 [18432, 4608], P('vocab', 'dp'), may hold values from -0.25 to 0.25
- new_mask: int32 [18432], P('vocab'), may hold values from 0 to 1, as said below
- labels: int32 [4, 2, 64], P('dp'), may hold values from 0 to 18431
- in_grad: bfloat16 [4, 2, 192, 4608], P('dp', None, 'vocab'), may hold values from -0.75 to 0.75
- item_owner: int32 [4, 2, 192, 1], P('dp', None, 'vocab'), may hold values from 0 to 7; in each aligned block of 24 rows (0 to 23, 24 to 47, ..., all dimensions but the last counted through in order) at most 6 rows name the same one
- item_slot: int32 [4, 2, 192], P('dp', None, 'vocab'), may hold values from 0 to 255
- first_moment: float32 [2048, 4608], P('vocab', 'dp'), may hold values from -0.75 to 0.75
- second_moment: float32 [2048, 4608], P('vocab', 'dp'), may hold values from 0.0001 to 0.01
Outputs:
- token_loss: float32 [4, 2, 64], P('dp')
- d_hidden: bfloat16 [4, 2, 64, 4608], P('dp', None, None, 'vocab')
- update: float32 [2048, 4608], P('vocab', 'dp')
- first_out: float32 [2048, 4608], P('vocab', 'dp')
- second_out: float32 [2048, 4608], P('vocab', 'dp')
Inputs may be any that keep to these rules, and one draw needn't show every extreme that they name: `new_mask`: each aligned block of 2304 entries holds exactly 256 ones. `item_owner`: within the 24 rows of one device in one block, no shard is named more than 6 times, a bound that some block reaches.
All inputs are finite; a program needn't handle non-finite values.
Results may differ from a plain program's by a relative error of at most 0.006.
Values may be sent and summed in bfloat16 or wider, within the bound.
A program may use at most 128 MiB of HBM per device.

v0:
```python
import jax
import jax.numpy as jnp
from jax import lax
from jax.sharding import PartitionSpec as P

cap_value = 30.0
beta_one = 0.9
beta_two = 0.95
step_count = 10
epsilon = 1e-08
decay_rate = 0.1


def as_sent(array):
    return jax.tree.map(lambda a: a.astype(jnp.bfloat16) if a.dtype == jnp.float32 else a, array)


def select_rows(new_mask, new_count):
    ranked = jnp.cumsum(new_mask) - 1
    wanted = (ranked[None, :] == jnp.arange(new_count, dtype=jnp.int32)[:, None]) & (
        new_mask[None, :] == 1
    )
    return wanted.astype(jnp.bfloat16)


def softmax_error(raw, label_row, vocab_start):
    capped = cap_value * jnp.tanh(raw / cap_value)
    expd = jnp.exp(capped)
    hits = jnp.arange(raw.shape[1], dtype=jnp.int32)[None, :] + vocab_start == label_row[:, None]
    local_total = jnp.sum(expd, axis=1)
    local_pick = jnp.sum(jnp.where(hits, capped, 0.0), axis=1)
    total, picked = lax.psum((local_total, local_pick), "vocab")
    loss = jnp.log(total) - picked
    error = (
        (expd / total[:, None] - hits.astype(jnp.float32)) * (1.0 - (capped / cap_value) ** 2)
    ).astype(jnp.bfloat16)
    return (loss, error)


def finish_hidden(partial_value):
    return lax.psum_scatter(partial_value, "vocab", scatter_dimension=1, tiled=True).astype(
        jnp.bfloat16
    )


def pack_items(rows, owner, slot, shards, capacity):
    onehot = (owner[:, None] == jnp.arange(shards, dtype=jnp.int32)[None, :]).astype(jnp.int32)
    running = jnp.cumsum(onehot, axis=0)
    ranked = jnp.sum(onehot * running, axis=1) - 1
    place = owner * capacity + ranked
    placing = jnp.arange(shards * capacity, dtype=jnp.int32)[:, None] == place[None, :]
    sent = jnp.dot(placing.astype(jnp.bfloat16), rows, preferred_element_type=jnp.float32).astype(
        jnp.bfloat16
    )
    targets = jnp.sum(placing.astype(jnp.int32) * (slot + 1)[None, :], axis=1) - 1
    return (sent.reshape(shards, capacity, rows.shape[1]), targets.reshape(shards, capacity))


def scatter_items(rows, targets, new_count):
    picking = (jnp.arange(new_count, dtype=jnp.int32)[:, None] == targets[None, :]).astype(
        jnp.bfloat16
    )
    return jnp.dot(picking, rows, preferred_element_type=jnp.float32)


def body(
    hidden, table, new_mask, labels, in_grad, item_owner, item_slot, first_moment, second_moment
):
    blocks = hidden.shape[1]
    width = hidden.shape[3]
    slice_width = table.shape[1]
    new_count = first_moment.shape[0]
    shards = lax.axis_size("vocab")
    groups = lax.axis_size("dp")
    items_here = in_grad.shape[2]
    capacity = max(2, (2 * items_here + shards - 1) // shards)
    vocab_start = lax.axis_index("vocab") * table.shape[0]
    select = select_rows(new_mask, new_count)
    params = jnp.dot(select, table, preferred_element_type=jnp.float32)
    received_rows = []
    received_targets = []
    losses = []
    dstates = []
    grads = jnp.zeros((new_count, slice_width), jnp.float32)
    for c in range(blocks):
        states = hidden[0, c]
        spread = lax.all_to_all(states, "dp", split_axis=1, concat_axis=0, tiled=True)
        raw = lax.psum_scatter(
            lax.dot_general(
                spread, table, (((1,), (1,)), ((), ())), preferred_element_type=jnp.float32
            ),
            "dp",
            scatter_dimension=0,
            tiled=True,
        )
        loss, error = softmax_error(raw, labels[0, c], vocab_start)
        piece = lax.all_gather(error, "dp", axis=0, tiled=True)
        part = jnp.dot(piece, table, preferred_element_type=jnp.float32)
        picked = lax.dot_general(
            piece, select, (((1,), (1,)), ((), ())), preferred_element_type=jnp.float32
        )
        joined = jnp.concatenate([part, picked], axis=1)
        chosen = joined[:, slice_width:].astype(jnp.bfloat16)
        grads = grads + lax.dot_general(
            chosen, spread, (((0,), (0,)), ((), ())), preferred_element_type=jnp.float32
        )
        regrouped = lax.all_to_all(
            joined[:, :slice_width], "dp", split_axis=0, concat_axis=1, tiled=True
        )
        dstates.append(finish_hidden(regrouped))
        losses.append(loss)
        sent_rows, sent_targets = pack_items(
            in_grad[0, c], item_owner[0, c, :, 0], item_slot[0, c], shards, capacity
        )
        got_rows, got_targets = (
            lax.all_to_all(sent_rows, "vocab", split_axis=0, concat_axis=0, tiled=True),
            lax.all_to_all(sent_targets, "vocab", split_axis=0, concat_axis=0, tiled=True),
        )
        received_rows.append(got_rows.reshape(-1, width))
        received_targets.append(got_targets.reshape(-1))
    item_rows = jnp.concatenate(received_rows, axis=0)
    item_targets = jnp.concatenate(received_targets, axis=0)
    tiled = jnp.broadcast_to(item_targets[:, None], (item_targets.shape[0], groups))
    slice_rows, slice_targets = (
        lax.all_to_all(item_rows, "dp", split_axis=1, concat_axis=0, tiled=True),
        lax.all_to_all(as_sent(tiled), "dp", split_axis=1, concat_axis=0, tiled=True).astype(
            tiled.dtype
        ),
    )
    grads = grads + scatter_items(slice_rows, slice_targets[:, 0], new_count)
    first_out = beta_one * first_moment + (1.0 - beta_one) * grads
    second_out = beta_two * second_moment + (1.0 - beta_two) * grads * grads
    update = (
        first_out
        / (1.0 - beta_one**step_count)
        / (jnp.sqrt(second_out / (1.0 - beta_two**step_count)) + epsilon)
        + decay_rate * params
    )
    token_loss = jnp.stack(losses)[None]
    d_hidden = jnp.stack(dstates)[None]
    return (token_loss, d_hidden, update, first_out, second_out)


def solution(mesh):
    return jax.shard_map(
        body,
        mesh=mesh,
        in_specs=(
            P("dp", None, None, None),
            P("vocab", "dp"),
            P("vocab"),
            P("dp", None, None),
            P("dp", None, "vocab", None),
            P("dp", None, "vocab", None),
            P("dp", None, "vocab"),
            P("vocab", "dp"),
            P("vocab", "dp"),
        ),
        out_specs=(
            P("dp", None, None),
            P("dp", None, None, "vocab"),
            P("vocab", "dp"),
            P("vocab", "dp"),
            P("vocab", "dp"),
        ),
        check_vma=False,
    )
```

profile of v0, /device:TPU:6, one launch (start us, length us, event | category | flops | bytes accessed | tf_op | source)
XLA Modules:
  0.0 351.0 jit_solution(7385280717842510813)
XLA Ops:
  8.8 20.6 %all_to_all.127 = bf16[64,4,1152]{2,0,1:T(8,128)(2,1)S(1)} all-to-all(bf16[64,4,1152]{2,0,1:T(8,128)(2,1)S(1)} %copy.31), channel_id=1, replica_groups=mesh['dp'=4,'vocab'=8] {'dp'}, dimensions={1} | all-to-all | bytes 1179648 | tf_op jit(solution)/shard_map/all_to_all | solution.py:87
  30.1 5.6 %fusion.47 = f32[256,2304]{1,0:T(8,128)} fusion(bf16[256,1152]{1,0:T(8,128)(2,1)S(1)} %bitcast.91, bf16[2304,1152]{1,0:T(8,128)(2,1)} %param.10), kind=kOutput, calls=%fused_computation.81 | convolution fusion | flops 1358954496 | bytes 8257536 | tf_op jit(solution)/shard_map/dot_general | solution.py:89
  36.1 33.2 %all_to_all.128 = bf16[64,4,1152]{2,0,1:T(8,128)(2,1)S(1)} all-to-all(bf16[64,4,1152]{2,0,1:T(8,128)(2,1)S(1)} %copy.32), channel_id=1, replica_groups=mesh['dp'=4,'vocab'=8] {'dp'}, dimensions={1} | all-to-all | bytes 1179648 | tf_op jit(solution)/shard_map/all_to_all | solution.py:87
  69.3 5.7 %fusion.48 = f32[256,2304]{1,0:T(8,128)} fusion(bf16[256,1152]{1,0:T(8,128)(2,1)S(1)} %bitcast.87, bf16[2304,1152]{1,0:T(8,128)(2,1)} %param.10), kind=kOutput, calls=%fused_computation.82 | convolution fusion | flops 1358954496 | bytes 8257536 | tf_op jit(solution)/shard_map/dot_general | solution.py:89
  75.8 13.7 %reduce-scatter.9.cloned.1.call-done = f32[64,2304]{1,0:T(8,128)} async-done(((f32[256,2304]{1,0:T(8,128)}), f32[64,2304]{1,0:T(8,128)}) %reduce-scatter.9.cloned.1.call-update) | async-done | bytes 589840 | tf_op jit(solution)/shard_map/reduce_scatter | solution.py:88
  89.5 51.9 %reduce-scatter.11.cloned.1.call-done = f32[64,2304]{1,0:T(8,128)} async-done(((f32[256,2304]{1,0:T(8,128)}), f32[64,2304]{1,0:T(8,128)}) %reduce-scatter.11.cloned.1.call-update) | async-done | bytes 589840 | tf_op jit(solution)/shard_map/reduce_scatter | solution.py:88
  143.3 10.7 %all-reduce = (f32[64]{0:T(128)S(1)}, f32[64]{0:T(128)S(1)}, f32[64]{0:T(128)}, f32[64]{0:T(128)S(1)}) all-reduce(f32[64]{0:T(128)S(1)} %get-tuple-element.19, f32[64]{0:T(128)S(1)} %get-tuple-element.20, f32[64]{0:T(128)S(1)} %get-tuple-element.6, f32[64]{0:T(128)S(1)} %get-tuple-element.5), channel_id=1, replica_groups=mesh['dp'=4,'vocab'=8] {'vocab'}, use_global_device_ids=true, to_apply=%region_9.10 | all-reduce | flops 256 | bytes 2048 | tf_op jit(solution)/shard_map/psum | solution.py:32
  156.4 7.2 %all-to-all-start.5 = ((s32[8,1,6]{2,1,0:T(1,128)}), s32[8,1,6]{2,1,0:T(1,128)S(1)}, u32[]{:S(2)}, u32[]{:S(2)}) async-start(s32[8,1,6]{2,1,0:T(1,128)} %bitcast.25), calls=%async_computation.7 | async-start | bytes 8192 | tf_op jit(solution)/shard_map/all_to_all | solution.py:117
  165.8 5.6 %all-to-all-start.4 = ((s32[8,1,6]{2,1,0:T(1,128)}), s32[8,1,6]{2,1,0:T(1,128)S(1)}, u32[]{:S(2)}, u32[]{:S(2)}) async-start(s32[8,1,6]{2,1,0:T(1,128)} %bitcast.22), calls=%async_computation.6 | async-start | bytes 8192 | tf_op jit(solution)/shard_map/all_to_all | solution.py:117
  179.9 4.1 %all-to-all-done.6 = s32[96,4,1]{0,2,1:T(1,128)S(1)} async-done(((s32[96,4,1]{0,2,1:T(1,128)}), s32[96,4,1]{0,2,1:T(1,128)S(1)}, u32[]{:S(2)}, u32[]{:S(2)}) %all-to-all-start.6) | async-done | bytes 1568 | tf_op jit(solution)/shard_map/all_to_all | solution.py:126
  184.0 5.8 %all-to-all-start.8 = ((bf16[8,6,4608]{2,1,0:T(8,128)(2,1)}), bf16[8,6,4608]{2,1,0:T(8,128)(2,1)S(1)}, u32[]{:S(2)}, u32[]{:S(2)}) async-start(bf16[8,6,4608]{2,1,0:T(8,128)(2,1)} %reshape.165), calls=%async_computation.10 | async-start | bytes 1179648 | tf_op jit(solution)/shard_map/all_to_all | solution.py:116
  191.2 6.7 %all-to-all-done.8 = bf16[8,6,4608]{2,1,0:T(8,128)(2,1)S(1)} async-done(((bf16[8,6,4608]{2,1,0:T(8,128)(2,1)}), bf16[8,6,4608]{2,1,0:T(8,128)(2,1)S(1)}, u32[]{:S(2)}, u32[]{:S(2)}) %all-to-all-start.8) | async-done | bytes 442400 | tf_op jit(solution)/shard_map/all_to_all | solution.py:116
  197.9 5.9 %all-to-all-start.7 = ((bf16[8,6,4608]{2,1,0:T(8,128)(2,1)}), bf16[8,6,4608]{2,1,0:T(8,128)(2,1)S(1)}, u32[]{:S(2)}, u32[]{:S(2)}) async-start(bf16[8,6,4608]{2,1,0:T(8,128)(2,1)} %reshape.164), calls=%async_computation.9 | async-start | bytes 1179648 | tf_op jit(solution)/shard_map/all_to_all | solution.py:116
  203.8 5.6 %fusion.50 = f32[256,1152]{1,0:T(8,128)} fusion(bf16[256,2304]{1,0:T(8,128)(2,1)} %all-gather.5.cloned.1.call-done, bf16[2304,1152]{1,0:T(8,128)(2,1)} %param.10), kind=kOutput, calls=%fused_computation.84 | convolution fusion | flops 1358954496 | bytes 7667712 | tf_op jit(solution)/shard_map/dot_general | solution.py:98
  216.2 4.9 %all-gather.3.cloned.1.call-done = bf16[256,2304]{1,0:T(8,128)(2,1)} async-done(((bf16[64,2304]{1,0:T(8,128)(2,1)}), bf16[256,2304]{1,0:T(8,128)(2,1)}) %all-gather.3.cloned.1.call-update) | async-done | bytes 1179664 | tf_op jit(solution)/shard_map/all_gather | solution.py:97
  221.1 5.6 %fusion.49 = f32[256,1152]{1,0:T(8,128)} fusion(bf16[256,2304]{1,0:T(8,128)(2,1)} %all-gather.3.cloned.1.call-done, bf16[2304,1152]{1,0:T(8,128)(2,1)} %param.10), kind=kOutput, calls=%fused_computation.83 | convolution fusion | flops 1358954496 | bytes 7667712 | tf_op jit(solution)/shard_map/dot_general | solution.py:98
  226.7 19.2 %all-to-all-done.3 = f32[4,64,1152]{2,1,0:T(8,128)S(1)} async-done(((f32[4,64,1152]{2,1,0:T(8,128)}), f32[4,64,1152]{2,1,0:T(8,128)S(1)}, u32[]{:S(2)}, u32[]{:S(2)}) %all-to-all-start.3) | async-done | bytes 1179680 | tf_op jit(solution)/shard_map/all_to_all | solution.py:107
  245.9 3.5 %all-to-all-start.2 = ((f32[4,64,1152]{2,1,0:T(8,128)}), f32[4,64,1152]{2,1,0:T(8,128)S(1)}, u32[]{:S(2)}, u32[]{:S(2)}) async-start(f32[4,64,1152]{2,1,0:T(8,128)} %bitcast.89), calls=%async_computation.4 | async-start | bytes 2359296 | tf_op jit(solution)/shard_map/all_to_all | solution.py:107
  254.3 24.0 %all-to-all-done.2 = f32[4,64,1152]{2,1,0:T(8,128)S(1)} async-done(((f32[4,64,1152]{2,1,0:T(8,128)}), f32[4,64,1152]{2,1,0:T(8,128)S(1)}, u32[]{:S(2)}, u32[]{:S(2)}) %all-to-all-start.2) | async-done | bytes 1179680 | tf_op jit(solution)/shard_map/all_to_all | solution.py:107
  284.7 18.9 %all-to-all-done.9 = bf16[96,4,1152]{2,0,1:T(8,128)(2,1)S(1)} async-done(((bf16[96,4,1152]{2,0,1:T(8,128)(2,1)}), bf16[96,4,1152]{2,0,1:T(8,128)(2,1)S(1)}, u32[]{:S(2)}, u32[]{:S(2)}) %all-to-all-start.9) | async-done | bytes 884768 | tf_op jit(solution)/shard_map/all_to_all | solution.py:125
  304.6 3.7 %fusion.22 = f32[256,1152]{1,0:T(8,128)} fusion(bf16[256,1152]{1,0:T(8,128)(2,1)} %bitcast.92, bf16[256,2304]{1,0:T(8,128)(2,1)} %all-gather.3.cloned.1.call-done, s32[2304]{0:T(1024)S(1)} %add_bitcast_fusion, pred[2304]{0:T(1024)(128)(4,1)S(1)} %broadcast_compare_fusion), kind=kOutput, calls=%fused_computation.21 | convolution fusion | flops 454230016 | bytes 2960640 | tf_op jit(solution)/shard_map/dot_general | solution.py:104
  308.3 4.8 %multiply_add_fusion = (f32[256,1152]{1,0:T(8,128)}, f32[256,1152]{1,0:T(8,128)}) fusion(f32[256,1152]{1,0:T(8,128)S(1)} %copy-done.4, f32[256,1152]{1,0:T(8,128)} %param.17, f32[256,1152]{1,0:T(8,128)S(1)} %fusion.34, f32[256,1152]{1,0:T(8,128)} %fusion.22, bf16[256,1152]{1,0:T(8,128)(2,1)S(1)} %bitcast.88, ...), kind=kOutput, calls=%fused_computation.12 | convolution fusion | flops 456884224 | bytes 8858880 | tf_op jit(solution)/shard_map/dot_general | solution.py:104
  313.2 6.3 %fusion.1 = f32[256,1152]{1,0:T(8,128)} fusion(bf16[2304,1152]{1,0:T(8,128)(2,1)} %param.10, f32[256,1152]{1,0:T(8,128)} %get-tuple-element.14, f32[256,1152]{1,0:T(8,128)} %get-tuple-element.13, s32[2304]{0:T(1024)S(1)} %add_bitcast_fusion, pred[2304]{0:T(1024)(128)(4,1)S(1)} %broadcast_compare_fusion), kind=kOutput, calls=%fused_computation.5 | convolution fusion | flops 1361903616 | bytes 8858880 | tf_op jit(solution)/shard_map/dot_general | solution.py:79
  320.5 21.8 %reduce-scatter.13.cloned.1.call-done = f32[576,64]{1,0:T(8,128)} async-done(((f32[4608,64]{1,0:T(8,128)}), f32[576,64]{1,0:T(8,128)}) %reduce-scatter.13.cloned.1.call-update) | async-done | bytes 147472
  (98 shorter events, 41.6 us)
Async XLA Ops:
  7.2 82.3 %reduce-scatter.9.cloned.1.call-start = ((), (), s32[]{:S(2)}) async-start(), calls=%async_computation.14 | async-start | bytes 2949120 | tf_op jit(solution)/shard_map/reduce_scatter | solution.py:88
  29.3 0.8 copy-start.5
  35.8 105.6 %reduce-scatter.11.cloned.1.call-start = ((), (), s32[]{:S(2)}) async-start(), calls=%async_computation.15 | async-start | bytes 2949120 | tf_op jit(solution)/shard_map/reduce_scatter | solution.py:88
  75.0 128.8 %all-gather.5.cloned.1.call-start = ((), (), s32[]{:S(2)}) async-start(), calls=%async_computation.17 | async-start | bytes 1474560 | tf_op jit(solution)/shard_map/all_gather | solution.py:97
  89.5 64.5 %copy-start.2 = (f32[64,2304]{1,0:T(8,128)S(1)}, f32[64,2304]{1,0:T(8,128)}, u32[]{:S(2)}) copy-start(f32[64,2304]{1,0:T(8,128)} %reduce-scatter.9.cloned.1.call-done) | copy-start | bytes 1769476
  141.4 12.6 %copy-start.3 = (f32[64,2304]{1,0:T(8,128)S(1)}, f32[64,2304]{1,0:T(8,128)}, u32[]{:S(2)}) copy-start(f32[64,2304]{1,0:T(8,128)} %reduce-scatter.11.cloned.1.call-done) | copy-start | bytes 1769476
  143.3 12.0 %copy-start.10 = (s32[1,2,24]{2,1,0:T(2,128)S(1)}, s32[1,2,24]{2,1,0:T(2,128)}, u32[]{:S(2)}) copy-start(s32[1,2,24]{2,1,0:T(2,128)} %param.15) | copy-start | bytes 580
  143.3 35.2 %copy-start.6 = (bf16[1,2,24,4608]{3,2,1,0:T(8,128)(2,1)S(1)}, bf16[1,2,24,4608]{3,2,1,0:T(8,128)(2,1)}, u32[]{:S(2)}) copy-start(bf16[1,2,24,4608]{3,2,1,0:T(8,128)(2,1)} %param.13) | copy-start | bytes 1327108
  156.4 9.4 %all-to-all-start.5 = ((s32[8,1,6]{2,1,0:T(1,128)}), s32[8,1,6]{2,1,0:T(1,128)S(1)}, u32[]{:S(2)}, u32[]{:S(2)}) async-start(s32[8,1,6]{2,1,0:T(1,128)} %bitcast.25), calls=%async_computation.7 | async-start | bytes 8192 | tf_op jit(solution)/shard_map/all_to_all | solution.py:117
  165.8 7.8 %all-to-all-start.4 = ((s32[8,1,6]{2,1,0:T(1,128)}), s32[8,1,6]{2,1,0:T(1,128)S(1)}, u32[]{:S(2)}, u32[]{:S(2)}) async-start(s32[8,1,6]{2,1,0:T(1,128)} %bitcast.22), calls=%async_computation.6 | async-start | bytes 8192 | tf_op jit(solution)/shard_map/all_to_all | solution.py:117
  175.1 8.9 %all-to-all-start.6 = ((s32[96,4,1]{0,2,1:T(1,128)}), s32[96,4,1]{0,2,1:T(1,128)S(1)}, u32[]{:S(2)}, u32[]{:S(2)}) async-start(s32[96,4,1]{0,2,1:T(1,128)} %broadcast_in_dim.14), calls=%async_computation.8 | async-start | bytes 4096 | tf_op jit(solution)/shard_map/all_to_all | solution.py:126
  184.0 13.9 %all-to-all-start.8 = ((bf16[8,6,4608]{2,1,0:T(8,128)(2,1)}), bf16[8,6,4608]{2,1,0:T(8,128)(2,1)S(1)}, u32[]{:S(2)}, u32[]{:S(2)}) async-start(bf16[8,6,4608]{2,1,0:T(8,128)(2,1)} %reshape.165), calls=%async_computation.10 | async-start | bytes 1179648 | tf_op jit(solution)/shard_map/all_to_all | solution.py:116
  189.8 31.2 %all-gather.3.cloned.1.call-start = ((), (), s32[]{:S(2)}) async-start(), calls=%async_computation.16 | async-start | bytes 1474560 | tf_op jit(solution)/shard_map/all_gather | solution.py:97
  197.9 13.9 %all-to-all-start.7 = ((bf16[8,6,4608]{2,1,0:T(8,128)(2,1)}), bf16[8,6,4608]{2,1,0:T(8,128)(2,1)S(1)}, u32[]{:S(2)}, u32[]{:S(2)}) async-start(bf16[8,6,4608]{2,1,0:T(8,128)(2,1)} %reshape.164), calls=%async_computation.9 | async-start | bytes 1179648 | tf_op jit(solution)/shard_map/all_to_all | solution.py:116
  211.8 0.8 copy-start
  212.6 33.2 %all-to-all-start.3 = ((f32[4,64,1152]{2,1,0:T(8,128)}), f32[4,64,1152]{2,1,0:T(8,128)S(1)}, u32[]{:S(2)}, u32[]{:S(2)}) async-start(f32[4,64,1152]{2,1,0:T(8,128)} %bitcast.90), calls=%async_computation.5 | async-start | bytes 2359296 | tf_op jit(solution)/shard_map/all_to_all | solution.py:107
  245.9 32.4 %all-to-all-start.2 = ((f32[4,64,1152]{2,1,0:T(8,128)}), f32[4,64,1152]{2,1,0:T(8,128)S(1)}, u32[]{:S(2)}, u32[]{:S(2)}) async-start(f32[4,64,1152]{2,1,0:T(8,128)} %bitcast.89), calls=%async_computation.4 | async-start | bytes 2359296 | tf_op jit(solution)/shard_map/all_to_all | solution.py:107
  249.4 70.0 %reduce-scatter.15.cloned.1.call-start = ((), (), s32[]{:S(2)}) async-start(), calls=%async_computation.19 | async-start | bytes 2654208
  251.4 1.1 copy-start.1
  254.3 27.8 %copy-start.7 = (s32[2304]{0:T(1024)S(1)}, s32[2304]{0:T(1024)}, u32[]{:S(2)}) copy-start(s32[2304]{0:T(1024)} %param.11) | copy-start | bytes 27652
  278.3 25.3 %all-to-all-start.9 = ((bf16[96,4,1152]{2,0,1:T(8,128)(2,1)}), bf16[96,4,1152]{2,0,1:T(8,128)(2,1)S(1)}, u32[]{:S(2)}, u32[]{:S(2)}) async-start(bf16[96,4,1152]{2,0,1:T(8,128)(2,1)} %copy.37), calls=%async_computation.11 | async-start | bytes 1769472 | tf_op jit(solution)/shard_map/all_to_all | solution.py:125
  281.8 60.5 %reduce-scatter.13.cloned.1.call-start = ((), (), s32[]{:S(2)}) async-start(), calls=%async_computation.18 | async-start | bytes 2654208
  284.6 19.4 %copy-start.11 = (f32[64]{0:T(128)S(1)}, f32[64]{0:T(128)}, u32[]{:S(2)}) copy-start(f32[64]{0:T(128)} %get-tuple-element.11) | copy-start | bytes 772
  304.6 3.7 %copy-start.4 = (f32[256,1152]{1,0:T(8,128)S(1)}, f32[256,1152]{1,0:T(8,128)}, u32[]{:S(2)}) copy-start(f32[256,1152]{1,0:T(8,128)} %param.16) | copy-start | bytes 3538948
  (2 other events, 1.4 us)
Sparse Core Ops, SparseCore 0:
  35.9 53.5 reduce-scatter.8
  91.8 49.5 reduce-scatter.10
  155.4 31.8 all-gather.4
  191.9 29.1 all-gather.2
  253.3 42.9 reduce-scatter.14
  299.8 42.4 reduce-scatter.12
where the time goes:
time: 354 us; the launch traced here: 351 us
  waiting for transfers between devices  170 us (48%)
  blocking collectives  64.4 us (18%)
  starting transfers between devices  38.9 us (11%)
  matrix products  38.6 us (11%)
  local copies, waits for them, and re-layouts  17.1 us (5%)
  between operations  14.3 us (4%)
  other arithmetic  7.52 us (2%)
    reduce_scatter x2, waiting for transfers between devices, body(): lax.psum_scatter(lax.dot_general(spread, table, (((1,), (1,)), ((), ())),...  65.5 us
    all_to_all x2, blocking collectives, body(): lax.all_to_all(states, 'dp', split_axis=1, concat_axis=0, tiled=True)  53.8 us
    all_to_all x2, waiting for transfers between devices, body(): lax.all_to_all(joined[:, :slice_width], 'dp', split_axis=0, concat_axis=1...  43.2 us
    unnamed x8, waiting for transfers between devices  21.9 us
    all_to_all x1, waiting for transfers between devices, body(): lax.all_to_all(item_rows, 'dp', split_axis=1, concat_axis=0, tiled=True)  18.9 us
    all_to_all x2, starting transfers between devices, body(): lax.all_to_all(sent_targets, 'vocab', split_axis=0, concat_axis=0, tiled=...  12.8 us
    all_to_all x2, starting transfers between devices, body(): lax.all_to_all(sent_rows, 'vocab', split_axis=0, concat_axis=0, tiled=True)  11.7 us
    dot_general x2, matrix products, body(): lax.dot_general(spread, table, (((1,), (1,)), ((), ())), preferred_elemen...  11.3 us
  transfers between devices with their start and end apart: 14, of which 12 were waited for; matrix products, arithmetic and copies ran while one was open for 14% of the time, Pallas kernels for 0%

commit v1 on v0

v1 whole, which is shorter than its diff:
```python
import jax
import jax.numpy as jnp
from jax import lax
from jax.sharding import PartitionSpec as P

cap_value = 30.0
beta_one = 0.9
beta_two = 0.95
step_count = 10
epsilon = 1e-08
decay_rate = 0.1


def select_rows(new_mask, new_count):
    ranked = jnp.cumsum(new_mask) - 1
    wanted = (ranked[None, :] == jnp.arange(new_count, dtype=jnp.int32)[:, None]) & (
        new_mask[None, :] == 1
    )
    return wanted.astype(jnp.bfloat16)


def softmax_error(raw, label_row, vocab_start):
    capped = cap_value * jnp.tanh(raw / cap_value)
    expd = jnp.exp(capped)
    hits = jnp.arange(raw.shape[1], dtype=jnp.int32)[None, :] + vocab_start == label_row[:, None]
    local_total = jnp.sum(expd, axis=1)
    local_pick = jnp.sum(jnp.where(hits, capped, 0.0), axis=1)
    total, picked = lax.psum(jnp.stack([local_total, local_pick]), "vocab")
    loss = jnp.log(total) - picked
    error = (
        (expd / total[:, None] - hits.astype(jnp.float32)) * (1.0 - (capped / cap_value) ** 2)
    ).astype(jnp.bfloat16)
    return (loss, error)


def gather_states(states, shards):
    share = states.shape[0] // shards
    mine = lax.dynamic_slice_in_dim(states, lax.axis_index("vocab") * share, share, 0)
    groups = lax.axis_size("dp")
    cut = lax.all_to_all(mine, "dp", split_axis=1, concat_axis=0, tiled=True)
    cut = cut.reshape(groups, share, -1)
    return lax.all_gather(cut, "vocab", axis=1, tiled=True).reshape(groups * share * shards, -1)


def finish_hidden(part, groups, shards):
    ratio = shards // groups
    mine = lax.psum_scatter(part.astype(jnp.bfloat16), "vocab", scatter_dimension=0, tiled=True)
    rows, columns = mine.shape
    pieces = mine.reshape(rows, ratio, columns // ratio).transpose(1, 0, 2)
    place = lax.rem(lax.axis_index("vocab"), ratio)
    got = []
    for r in range(ratio):
        pairs = [
            (d * shards + v, (v // ratio) * shards + ratio * d + (v % ratio + r) % ratio)
            for d in range(groups)
            for v in range(shards)
        ]
        piece = lax.dynamic_index_in_dim(pieces, lax.rem(place + r, ratio), 0, keepdims=False)
        got.append(lax.ppermute(piece, ("dp", "vocab"), pairs))
    order = lax.rem(place - jnp.arange(ratio, dtype=jnp.int32) + ratio, ratio)
    return jnp.stack(got)[order].reshape(ratio * rows, columns // ratio)


def pack_items(rows, owner, slot, shards, capacity, groups):
    onehot = (owner[:, None] == jnp.arange(shards, dtype=jnp.int32)[None, :]).astype(jnp.int32)
    running = jnp.cumsum(onehot, axis=0)
    ranked = jnp.sum(onehot * running, axis=1) - 1
    place = owner * capacity + ranked
    placing = jnp.arange(shards * capacity, dtype=jnp.int32)[:, None] == place[None, :]
    sent = jnp.dot(placing.astype(jnp.bfloat16), rows, preferred_element_type=jnp.float32).astype(
        jnp.bfloat16
    )
    targets = jnp.sum(placing.astype(jnp.int32) * (slot + 1)[None, :], axis=1)
    sent = sent.reshape(shards, capacity, groups, -1).transpose(2, 0, 1, 3)
    high, low = (targets // 128).astype(jnp.bfloat16), (targets % 128).astype(jnp.bfloat16)
    code = jnp.stack([high, low], axis=1).reshape(1, shards, capacity, 2)
    code = jnp.broadcast_to(jnp.pad(code, ((0, 0), (0, 0), (0, 0), (0, 126))), (groups, shards, capacity, 128))
    return jnp.concatenate([sent, code], axis=3)


def scatter_items(rows, targets, new_count):
    picking = (jnp.arange(new_count, dtype=jnp.int32)[:, None] == targets[None, :]).astype(
        jnp.bfloat16
    )
    return jnp.dot(picking, rows, preferred_element_type=jnp.float32)


def body(
    hidden, table, new_mask, labels, in_grad, item_owner, item_slot, first_moment, second_moment
):
    blocks, span, width = hidden.shape[1:]
    slice_width = table.shape[1]
    new_count = first_moment.shape[0]
    shards = lax.axis_size("vocab")
    groups = lax.axis_size("dp")
    items_here = in_grad.shape[2]
    capacity = max(2, (2 * items_here + shards - 1) // shards)
    vocab_start = lax.axis_index("vocab") * table.shape[0]
    spread = gather_states(hidden.reshape(blocks * span, width), shards)
    packed = jnp.concatenate(
        [
            pack_items(
                in_grad[0, c], item_owner[0, c, :, 0], item_slot[0, c], shards, capacity, groups
            )
            for c in range(blocks)
        ],
        axis=2,
    ).reshape(groups * shards, blocks * capacity, slice_width + 128)
    got = lax.all_to_all(packed, ("dp", "vocab"), split_axis=0, concat_axis=0, tiled=True)
    got = got.reshape(-1, slice_width + 128)
    targets = (
        got[:, slice_width].astype(jnp.int32) * 128 + got[:, slice_width + 1].astype(jnp.int32) - 1
    )
    in_sum = scatter_items(got[:, :slice_width], targets, new_count)
    select = select_rows(new_mask, new_count)
    params = jnp.dot(select, table, preferred_element_type=jnp.float32)
    partial_raw = lax.dot_general(
        spread, table, (((1,), (1,)), ((), ())), preferred_element_type=jnp.float32
    ).astype(jnp.bfloat16)
    raw = lax.psum_scatter(partial_raw, "dp", scatter_dimension=0, tiled=True)
    loss, error = softmax_error(raw.astype(jnp.float32), labels.reshape(-1), vocab_start)
    piece = lax.all_gather(error, "dp", axis=0, tiled=True)
    part = jnp.dot(piece, table, preferred_element_type=jnp.float32)
    d_hidden = finish_hidden(part, groups, shards)
    chosen = lax.dot_general(
        piece, select, (((1,), (1,)), ((), ())), preferred_element_type=jnp.float32
    ).astype(jnp.bfloat16)
    grads = in_sum + lax.dot_general(
        chosen, spread, (((0,), (0,)), ((), ())), preferred_element_type=jnp.float32
    )
    first_out = beta_one * first_moment + (1.0 - beta_one) * grads
    second_out = beta_two * second_moment + (1.0 - beta_two) * grads * grads
    update = (
        first_out
        / (1.0 - beta_one**step_count)
        / (jnp.sqrt(second_out / (1.0 - beta_two**step_count)) + epsilon)
        + decay_rate * params
    )
    return (
        loss.reshape(1, blocks, span),
        d_hidden.reshape(1, blocks, span, -1),
        update,
        first_out,
        second_out,
    )


def solution(mesh):
    return jax.shard_map(
        body,
        mesh=mesh,
        in_specs=(
            P("dp", None, None, None),
            P("vocab", "dp"),
            P("vocab"),
            P("dp", None, None),
            P("dp", None, "vocab", None),
            P("dp", None, "vocab", None),
            P("dp", None, "vocab"),
            P("vocab", "dp"),
            P("vocab", "dp"),
        ),
        out_specs=(
            P("dp", None, None),
            P("dp", None, None, "vocab"),
            P("vocab", "dp"),
            P("vocab", "dp"),
            P("vocab", "dp"),
        ),
        check_vma=False,
    )
```

time: 354 us -> 262 us (0.74)
  blocking collectives: 64.4 us -> 21.3 us
  starting transfers between devices: 38.9 us -> 13.5 us
  matrix products: 38.6 us -> 28.7 us
  waiting for transfers between devices: 170 us -> 163 us
    all_to_all x8 -> x1, waiting for transfers between devices: 77.8 us -> 0.01 us  [body(): lax.all_to_all(packed, ('dp', 'vocab'), split_axis=0, concat_axis=0, tile...]
    all_gather x2 -> x1, waiting for transfers between devices: 4.88 us -> 68.4 us  [body(): piece = lax.all_gather(error, 'dp', axis=0, tiled=True)]
    all_to_all x2 -> x1, blocking collectives: 53.8 us -> 11.3 us  [gather_states(): cut = lax.all_to_all(mine, 'dp', split_axis=1, concat_axis=0, tiled=True)]
    all_to_all x8 -> x1, starting transfers between devices: 38.5 us -> 6.42 us  [body(): lax.all_to_all(packed, ('dp', 'vocab'), split_axis=0, concat_axis=0, tile...]
    all_gather x0 -> x1, waiting for transfers between devices: none -> 22 us  [gather_states(): lax.all_gather(cut, 'vocab', axis=1, tiled=True)]
    unnamed x8 -> x4, waiting for transfers between devices: 21.9 us -> 0.07 us
    ppermute x0 -> x2, starting transfers between devices: none -> 6.93 us  [finish_hidden(): got.append(lax.ppermute(piece, ('dp', 'vocab'), pairs))]
    reduce_scatter x2, waiting for transfers between devices: 65.5 us -> 71.2 us  [the longest x1 48.4 us: body(): raw = lax.psum_scatter(partial_raw, 'dp', scatter_dimension=0, tiled=True)]
  transfers between devices with their start and end apart: 14 -> 7, of which waited for: 12 -> 5; matrix products, arithmetic and copies ran while one was open for 14% -> 11% of each run, Pallas kernels for 0% -> 0%
where the time goes in v1:
time: 262 us; the launch traced here: 261 us
  waiting for transfers between devices  163 us (62%)
  matrix products  28.7 us (11%)
  blocking collectives  21.3 us (8%)
  local copies, waits for them, and re-layouts  14.1 us (5%)
  between operations  14.1 us (5%)
  starting transfers between devices  13.5 us (5%)
  other arithmetic  5.67 us (2%)
    all_gather x1, waiting for transfers between devices, body(): piece = lax.all_gather(error, 'dp', axis=0, tiled=True)  68.4 us
    reduce_scatter x1, waiting for transfers between devices, body(): raw = lax.psum_scatter(partial_raw, 'dp', scatter_dimension=0, tiled=True)  48.4 us
    reduce_scatter x1, waiting for transfers between devices, finish_hidden(): lax.psum_scatter(part.astype(jnp.bfloat16), 'vocab', scatter_dimension=0,...  22.8 us
    all_gather x1, waiting for transfers between devices, gather_states(): lax.all_gather(cut, 'vocab', axis=1, tiled=True)  22 us
    all_to_all x1, blocking collectives, gather_states(): cut = lax.all_to_all(mine, 'dp', split_axis=1, concat_axis=0, tiled=True)  11.3 us
    psum x1, blocking collectives, softmax_error(): total, picked = lax.psum(jnp.stack([local_total, local_pick]), 'vocab')  10 us
    dot_general x1, matrix products, body(): part = jnp.dot(piece, table, preferred_element_type=jnp.float32)  7.45 us
    dot_general x1, matrix products, body(): lax.dot_general(spread, table, (((1,), (1,)), ((), ())), preferred_elemen...  7.1 us
  transfers between devices with their start and end apart: 7, of which 5 were waited for; matrix products, arithmetic and copies ran while one was open for 11% of the time, Pallas kernels for 0%

profile of v1, /device:TPU:6, one launch (start us, length us, event | category | flops | bytes accessed | tf_op | source)
XLA Modules:
  0.0 260.6 jit_solution(5262031433439252954)
XLA Ops:
  7.2 1.2 copy-done
  8.5 11.3 %all_to_all.21 = bf16[16,4,1152]{2,0,1:T(8,128)(2,1)S(1)} all-to-all(bf16[16,4,1152]{2,0,1:T(8,128)(2,1)S(1)} %bitcast.64), channel_id=1, replica_groups=mesh['dp'=4,'vocab'=8] {'dp'}, dimensions={1} | all-to-all | bytes 294912 | tf_op jit(solution)/shard_map/all_to_all | solution.py:40
  20.6 22.0 %all-gather.3.cloned.1.call-done = bf16[4,128,1152]{2,0,1:T(4,128)(2,1)} async-done(((bf16[4,16,1152]{2,0,1:T(4,128)(2,1)}), bf16[4,128,1152]{2,0,1:T(4,128)(2,1)}) %all-gather.3.cloned.1.call-update) | async-done | bytes 1179664 | tf_op jit(solution)/shard_map/all_gather | solution.py:42
  42.6 1.4 copy.53
  45.1 7.1 %convolution_convert_fusion.2 = bf16[512,2304]{1,0:T(8,128)(2,1)} fusion(bf16[512,1152]{1,0:T(8,128)(2,1)S(1)} %bitcast.61, bf16[2304,1152]{1,0:T(8,128)(2,1)} %param.10), kind=kOutput, calls=%fused_computation.3 | convolution fusion | flops 2719088640 | bytes 8847360 | tf_op jit(solution)/shard_map/dot_general | solution.py:117
  52.9 48.4 %reduce-scatter.3.cloned.1.call-done = bf16[128,2304]{1,0:T(8,128)(2,1)} async-done(((bf16[512,2304]{1,0:T(8,128)(2,1)}), bf16[128,2304]{1,0:T(8,128)(2,1)}) %reduce-scatter.3.cloned.1.call-update) | async-done | bytes 589840 | tf_op jit(solution)/shard_map/reduce_scatter | solution.py:120
  101.3 1.7 fusion.17
  103.1 10.0 %psum.7 = f32[2,128]{1,0:T(2,128)S(1)} all-reduce(f32[2,128]{1,0:T(2,128)S(1)} %pad_maximum_fusion.1), channel_id=1, replica_groups=mesh['dp'=4,'vocab'=8] {'vocab'}, use_global_device_ids=true, to_apply=%region_3.4 | all-reduce | flops 256 | bytes 2048 | tf_op jit(solution)/shard_map/psum | solution.py:28
  113.7 1.4 fusion.11
  117.8 1.6 copy.60
  119.4 6.4 %all-to-all-start.1 = ((bf16[32,12,1280]{2,1,0:T(8,128)(2,1)}), bf16[32,12,1280]{2,1,0:T(8,128)(2,1)S(1)}, u32[]{:S(2)}, u32[]{:S(2)}) async-start(bf16[32,12,1280]{2,1,0:T(8,128)(2,1)} %copy.60), calls=%async_computation.3 | async-start | bytes 2621440 | tf_op jit(solution)/shard_map/all_to_all | solution.py:109
  126.3 68.4 %all-gather.5.cloned.1.call-done = bf16[512,2304]{1,0:T(8,128)(2,1)} async-done(((bf16[128,2304]{1,0:T(8,128)(2,1)}), bf16[512,2304]{1,0:T(8,128)(2,1)}) %all-gather.5.cloned.1.call-update) | async-done | bytes 2359312 | tf_op jit(solution)/shard_map/all_gather | solution.py:122
  194.7 7.4 %convolution_convert_fusion.3 = bf16[512,1152]{1,0:T(8,128)(2,1)} fusion(bf16[512,2304]{1,0:T(8,128)(2,1)} %all-gather.5.cloned.1.call-done, bf16[2304,1152]{1,0:T(8,128)(2,1)} %param.10), kind=kOutput, calls=%fused_computation.4 | convolution fusion | flops 2718498816 | bytes 8847360 | tf_op jit(solution)/shard_map/dot_general | solution.py:123
  204.0 1.1 copy.65
  205.2 1.6 fusion.22
  206.9 1.3 sub.64
  208.2 5.9 %multiply_add_fusion = (f32[256,1152]{1,0:T(8,128)}, f32[256,1152]{1,0:T(8,128)}) fusion(f32[256,1152]{1,0:T(8,128)} %param.16, f32[256,1152]{1,0:T(8,128)} %param.17, f32[256,1152]{1,0:T(8,128)S(1)} %fusion.22, bf16[512,1152]{1,0:T(8,128)(2,1)S(1)} %bitcast.62, bf16[512,2304]{1,0:T(8,128)(2,1)} %all-gather.5.cloned.1.call-done, ...), kind=kOutput, calls=%fused_computation.20 | convolution fusion | flops 909639680 | bytes 9448704 | tf_op jit(solution)/shard_map/dot_general | solution.py:128
  214.1 22.8 %reduce-scatter.5.cloned.1.call-done = bf16[64,1152]{1,0:T(8,128)(2,1)} async-done(((bf16[512,1152]{1,0:T(8,128)(2,1)}), bf16[64,1152]{1,0:T(8,128)(2,1)}) %reduce-scatter.5.cloned.1.call-update) | async-done | bytes 147472 | tf_op jit(solution)/shard_map/reduce_scatter | solution.py:47
  236.9 1.1 reshape.417
  238.4 3.6 %collective-permute-start.1 = (bf16[64,576]{1,0:T(8,128)(2,1)S(1)}, bf16[64,576]{1,0:T(8,128)(2,1)S(1)}, u32[]{:S(2)}, u32[]{:S(2)}) collective-permute-start(bf16[64,576]{1,0:T(8,128)(2,1)S(1)} %bitcast.70), channel_id=1, source_target_pairs={{0,1},{1,0},{2,9},{3,8},{4,17},{5,16},{6,25},{7,24},{8,3},{9,2},{1... | collective-permute-start | bytes 221192 | tf_op jit(solution)/shard_map/ppermute | solution.py:59
  242.0 3.3 %collective-permute-start = (bf16[64,576]{1,0:T(8,128)(2,1)S(1)}, bf16[64,576]{1,0:T(8,128)(2,1)S(1)}, u32[]{:S(2)}, u32[]{:S(2)}) collective-permute-start(bf16[64,576]{1,0:T(8,128)(2,1)S(1)} %bitcast.69), channel_id=1, source_target_pairs={{0,0},{1,1},{2,8},{3,9},{4,16},{5,17},{6,24},{7,25},{8,2},{9,3},{1... | collective-permute-start | bytes 221192 | tf_op jit(solution)/shard_map/ppermute | solution.py:59
  245.3 5.9 %fusion = f32[256,1152]{1,0:T(8,128)} fusion(bf16[2304,1152]{1,0:T(8,128)(2,1)} %param.10, f32[256,1152]{1,0:T(8,128)} %get-tuple-element.8, f32[256,1152]{1,0:T(8,128)S(1)} %copy-done.4, s32[2304]{0:T(1024)S(1)} %add_bitcast_fusion, pred[2304]{0:T(1024)(128)(4,1)S(1)} %broadcast_compare_fusion), kind=kOutput, calls=%fused_computation.7 | convolution fusion | flops 1361903616 | bytes 8858880 | tf_op jit(solution)/shard_map/dot_general | solution.py:116
  251.2 1.5 collective-permute-done
  252.8 1.4 gather_fusion
  (80 shorter events, 8.6 us)
Async XLA Ops:
  7.2 1.3 copy-start
  7.2 35.5 %all-gather.3.cloned.1.call-start = ((), (), s32[]{:S(2)}) async-start(), calls=%async_computation.4 | async-start | bytes 1327104 | tf_op jit(solution)/shard_map/all_gather | solution.py:42
  20.6 80.8 %reduce-scatter.3.cloned.1.call-start = ((), (), s32[]{:S(2)}) async-start(), calls=%async_computation.5 | async-start | bytes 2949120 | tf_op jit(solution)/shard_map/reduce_scatter | solution.py:120
  44.0 1.0 copy-start.1
  52.2 0.7 copy-start.10
  52.2 0.8 copy-start.8
  52.2 142.5 %all-gather.5.cloned.1.call-start = ((), (), s32[]{:S(2)}) async-start(), calls=%async_computation.6 | async-start | bytes 2949120 | tf_op jit(solution)/shard_map/all_gather | solution.py:122
  101.3 12.4 %copy-start.5 = (bf16[128,2304]{1,0:T(8,128)(2,1)S(1)}, bf16[128,2304]{1,0:T(8,128)(2,1)}, u32[]{:S(2)}) copy-start(bf16[128,2304]{1,0:T(8,128)(2,1)} %reduce-scatter.3.cloned.1.call-done) | copy-start | bytes 1769476
  103.1 12.6 %copy-start.9 = (s32[1,2,24]{2,1,0:T(2,128)S(1)}, s32[1,2,24]{2,1,0:T(2,128)}, u32[]{:S(2)}) copy-start(s32[1,2,24]{2,1,0:T(2,128)} %param.15) | copy-start | bytes 580
  115.1 1.4 copy-start.6
  119.4 6.5 %copy-start.7 = (s32[2304]{0:T(1024)S(1)}, s32[2304]{0:T(1024)}, u32[]{:S(2)}) copy-start(s32[2304]{0:T(1024)} %param.11) | copy-start | bytes 27652
  119.4 83.6 %all-to-all-start.1 = ((bf16[32,12,1280]{2,1,0:T(8,128)(2,1)}), bf16[32,12,1280]{2,1,0:T(8,128)(2,1)S(1)}, u32[]{:S(2)}, u32[]{:S(2)}) async-start(bf16[32,12,1280]{2,1,0:T(8,128)(2,1)} %copy.60), calls=%async_computation.3 | async-start | bytes 2621440 | tf_op jit(solution)/shard_map/all_to_all | solution.py:109
  125.8 111.1 %reduce-scatter.5.cloned.1.call-start = ((), (), s32[]{:S(2)}) async-start(), calls=%async_computation.7 | async-start | bytes 1327104 | tf_op jit(solution)/shard_map/reduce_scatter | solution.py:47
  203.2 2.0 copy-start.3
  204.0 4.2 %copy-start.2 = (bf16[4,128,1152]{2,1,0:T(8,128)(2,1)S(1)}, bf16[4,128,1152]{2,1,0:T(8,128)(2,1)}, u32[]{:S(2)}) copy-start(bf16[4,128,1152]{2,1,0:T(8,128)(2,1)} %copy-done.1) | copy-start | bytes 3538948
  214.1 31.2 %copy-start.4 = (f32[256,1152]{1,0:T(8,128)S(1)}, f32[256,1152]{1,0:T(8,128)}, u32[]{:S(2)}) copy-start(f32[256,1152]{1,0:T(8,128)} %get-tuple-element.7) | copy-start | bytes 3538948
  238.4 12.8 %collective-permute-start.1 = (bf16[64,576]{1,0:T(8,128)(2,1)S(1)}, bf16[64,576]{1,0:T(8,128)(2,1)S(1)}, u32[]{:S(2)}, u32[]{:S(2)}) collective-permute-start(bf16[64,576]{1,0:T(8,128)(2,1)S(1)} %bitcast.70), channel_id=1, source_target_pairs={{0,1},{1,0},{2,9},{3,8},{4,17},{5,16},{6,25},{7,24},{8,3},{9,2},{1... | collective-permute-start | bytes 221192 | tf_op jit(solution)/shard_map/ppermute | solution.py:59
  242.0 10.7 %collective-permute-start = (bf16[64,576]{1,0:T(8,128)(2,1)S(1)}, bf16[64,576]{1,0:T(8,128)(2,1)S(1)}, u32[]{:S(2)}, u32[]{:S(2)}) collective-permute-start(bf16[64,576]{1,0:T(8,128)(2,1)S(1)} %bitcast.69), channel_id=1, source_target_pairs={{0,0},{1,1},{2,8},{3,9},{4,16},{5,17},{6,24},{7,25},{8,2},{9,3},{1... | collective-permute-start | bytes 221192 | tf_op jit(solution)/shard_map/ppermute | solution.py:59
Sparse Core Ops, SparseCore 0:
  20.7 21.9 all-gather.2
  52.3 48.9 reduce-scatter.2
  115.2 79.4 all-gather.4
  202.3 34.5 reduce-scatter.4

commit v2 on v1

--- a/solution.py
+++ b/solution.py
@@ -1,6 +1,10 @@
+import functools
+
 import jax
 import jax.numpy as jnp
 from jax import lax
+from jax.experimental import pallas as pl
+from jax.experimental.pallas import tpu as pltpu
 from jax.sharding import PartitionSpec as P
 
 cap_value = 30.0
@@ -19,18 +23,204 @@
     return wanted.astype(jnp.bfloat16)
 
 
-def softmax_error(raw, label_row, vocab_start):
-    capped = cap_value * jnp.tanh(raw / cap_value)
+MESH = pl.DeviceIdType.MESH
+
+
+def error_kernel(
+    groups,
+    shards,
+    raw_ref,
+    label_ref,
+    table_ref,
+    loss_ref,
+    piece_ref,
+    sum_ref,
+    stats,
+    square,
+    part,
+    inbox,
+    stat_send,
+    stat_recv,
+    line_send,
+    line_recv,
+    sum_send,
+    sum_recv,
+):
+    z = lax.axis_index("dp")
+    me = lax.axis_index("vocab")
+    tokens, rows_here = raw_ref.shape
+    chunk_rows = sum_ref.shape[0]
+    ratio = shards // groups
+    halves = 2
+    half = tokens // halves
+
+    barrier = pltpu.get_barrier_semaphore()
+    for k in range(1, shards):
+        pl.semaphore_signal(
+            barrier, inc=1, device_id={"vocab": lax.rem(me + k, shards)}, device_id_type=MESH
+        )
+
+    @pl.when(z < groups - 1)
+    def _():
+        pl.semaphore_signal(barrier, inc=1, device_id={"dp": z + 1}, device_id_type=MESH)
+
+    @pl.when(z > 0)
+    def _():
+        pl.semaphore_signal(barrier, inc=1, device_id={"dp": z - 1}, device_id_type=MESH)
+
+    capped = cap_value * jnp.tanh(raw_ref[...].astype(jnp.float32) / cap_value)
     expd = jnp.exp(capped)
-    hits = jnp.arange(raw.shape[1], dtype=jnp.int32)[None, :] + vocab_start == label_row[:, None]
-    local_total = jnp.sum(expd, axis=1)
-    local_pick = jnp.sum(jnp.where(hits, capped, 0.0), axis=1)
-    total, picked = lax.psum(jnp.stack([local_total, local_pick]), "vocab")
-    loss = jnp.log(total) - picked
-    error = (
-        (expd / total[:, None] - hits.astype(jnp.float32)) * (1.0 - (capped / cap_value) ** 2)
-    ).astype(jnp.bfloat16)
-    return (loss, error)
+    ids = lax.broadcasted_iota(jnp.int32, (tokens, rows_here), 1) + me * rows_here
+    hits = ids == label_ref[...]
+    local_total = jnp.sum(expd, axis=1, keepdims=True)
+    local_pick = jnp.sum(jnp.where(hits, capped, 0.0), axis=1, keepdims=True)
+    lane = lax.broadcasted_iota(jnp.int32, (tokens, 128), 1)
+    square[...] = jnp.where(lane == 0, local_total, jnp.where(lane == 1, local_pick, 0.0)).T
+    stats[0] = square[0:8, :]
+
+    near = (z < groups - 1).astype(jnp.int32) + (z > 0).astype(jnp.int32)
+    pl.semaphore_wait(barrier, shards - 1 + near)
+
+    def stat_copy(k):
+        return pltpu.make_async_remote_copy(
+            src_ref=stats.at[0],
+            dst_ref=stats.at[k],
+            send_sem=stat_send.at[k],
+            recv_sem=stat_recv.at[k],
+            device_id={"vocab": lax.rem(me + k, shards)},
+            device_id_type=MESH,
+        )
+
+    for k in range(1, shards):
+        stat_copy(k).start()
+    gathered = stats[0]
+    for k in range(1, shards):
+        stat_copy(k).wait_recv()
+        gathered = gathered + stats[k]
+    square[0:8, :] = gathered
+    columns = square[...].T
+    total = columns[:, 0:1]
+    loss_ref[...] = jnp.log(total) - columns[:, 1:2]
+    error = (expd / total - hits.astype(jnp.float32)) * (1.0 - (capped / cap_value) ** 2)
+    piece_ref[z] = error.astype(jnp.bfloat16)
+    for k in range(1, shards):
+        stat_copy(k).wait_send()
+
+    def line_copy(way, s, p, block, target):
+        place = piece_ref.at[block, pl.ds(p * half, half)]
+        return pltpu.make_async_remote_copy(
+            src_ref=place,
+            dst_ref=place,
+            send_sem=line_send.at[way, s, p],
+            recv_sem=line_recv.at[way, s, p],
+            device_id={"dp": target},
+            device_id_type=MESH,
+        )
+
+    def held(way, s):
+        return (z - s, z - s >= 0) if way == 0 else (z + s, z + s < groups)
+
+    def onward(way):
+        return (z + 1, z < groups - 1) if way == 0 else (z - 1, z > 0)
+
+    def sum_copy(chunk):
+        return pltpu.make_async_remote_copy(
+            src_ref=part.at[chunk],
+            dst_ref=inbox.at[me],
+            send_sem=sum_send.at[chunk],
+            recv_sem=sum_recv.at[me],
+            device_id={"vocab": chunk},
+            device_id_type=MESH,
+        )
+
+    for s in range(groups):
+        for p in range(halves):
+            for way in range(2):
+                block, have = held(way, s)
+                target, more = onward(way)
+                if s > 0:
+
+                    @pl.when(have)
+                    def _(way=way, s=s, p=p, block=block):
+                        line_copy(way, s - 1, p, block, z).wait_recv()
+
+                if s < groups - 1:
+
+                    @pl.when(have & more)
+                    def _(way=way, s=s, p=p, block=block, target=target):
+                        line_copy(way, s, p, block, target).start()
+
+        @pl.loop(0, 1 if s == 0 else 2)
+        def _(way, s=s):
+            block = z + s * (2 * way - 1)
+
+            @pl.when((block >= 0) & (block < groups))
+            def _():
+                product = jnp.dot(
+                    piece_ref[block], table_ref[...], preferred_element_type=jnp.float32
+                ).astype(jnp.bfloat16)
+                for b in range(ratio):
+                    chunk = block * ratio + b
+                    part[chunk] = product[b * chunk_rows : (b + 1) * chunk_rows]
+
+                    @pl.when(chunk != me)
+                    def _(chunk=chunk):
+                        sum_copy(chunk).start()
+
+    summed = part[me].astype(jnp.float32)
+    for k in range(1, shards):
+        source = lax.rem(me + k, shards)
+        pltpu.make_async_remote_copy(
+            src_ref=part.at[source],
+            dst_ref=inbox.at[source],
+            send_sem=sum_send.at[source],
+            recv_sem=sum_recv.at[source],
+            device_id={"vocab": source},
+            device_id_type=MESH,
+        ).wait()
+        summed = summed + inbox[source].astype(jnp.float32)
+    sum_ref[...] = summed.astype(jnp.bfloat16)
+    for s in range(groups - 1):
+        for p in range(halves):
+            for way in range(2):
+                block, have = held(way, s)
+                target, more = onward(way)
+
+                @pl.when(have & more)
+                def _(way=way, s=s, p=p, block=block, target=target):
+                    line_copy(way, s, p, block, target).wait_send()
+
+
+def error_and_sums(raw, labels, table, groups, shards):
+    tokens, rows_here = raw.shape
+    slice_width = table.shape[1]
+    chunk_rows = groups * tokens // shards
+    vmem = pl.BlockSpec(memory_space=pltpu.VMEM)
+    return pl.pallas_call(
+        functools.partial(error_kernel, groups, shards),
+        out_shape=(
+            jax.ShapeDtypeStruct((tokens, 1), jnp.float32),
+            jax.ShapeDtypeStruct((groups, tokens, rows_here), jnp.bfloat16),
+            jax.ShapeDtypeStruct((chunk_rows, slice_width), jnp.bfloat16),
+        ),
+        in_specs=[vmem] * 3,
+        out_specs=(vmem,) * 3,
+        scratch_shapes=[
+            pltpu.VMEM((shards, 8, tokens), jnp.float32),
+            pltpu.VMEM((128, tokens), jnp.float32),
+            pltpu.VMEM((shards, chunk_rows, slice_width), jnp.bfloat16),
+            pltpu.VMEM((shards, chunk_rows, slice_width), jnp.bfloat16),
+            pltpu.SemaphoreType.DMA((shards,)),
+            pltpu.SemaphoreType.DMA((shards,)),
+            pltpu.SemaphoreType.DMA((2, groups, 2)),
+            pltpu.SemaphoreType.DMA((2, groups, 2)),
+            pltpu.SemaphoreType.DMA((shards,)),
+            pltpu.SemaphoreType.DMA((shards,)),
+        ],
+        compiler_params=pltpu.CompilerParams(
+            collective_id=0, has_side_effects=True, vmem_limit_bytes=48 * 1024 * 1024
+        ),
+    )(raw, labels, table)
 
 
 def gather_states(states, shards):
@@ -42,9 +232,8 @@
     return lax.all_gather(cut, "vocab", axis=1, tiled=True).reshape(groups * share * shards, -1)
 
 
-def finish_hidden(part, groups, shards):
+def finish_hidden(mine, groups, shards):
     ratio = shards // groups
-    mine = lax.psum_scatter(part.astype(jnp.bfloat16), "vocab", scatter_dimension=0, tiled=True)
     rows, columns = mine.shape
     pieces = mine.reshape(rows, ratio, columns // ratio).transpose(1, 0, 2)
     place = lax.rem(lax.axis_index("vocab"), ratio)
@@ -95,7 +284,6 @@
     groups = lax.axis_size("dp")
     items_here = in_grad.shape[2]
     capacity = max(2, (2 * items_here + shards - 1) // shards)
-    vocab_start = lax.axis_index("vocab") * table.shape[0]
     spread = gather_states(hidden.reshape(blocks * span, width), shards)
     packed = jnp.concatenate(
         [
@@ -108,20 +296,20 @@
     ).reshape(groups * shards, blocks * capacity, slice_width + 128)
     got = lax.all_to_all(packed, ("dp", "vocab"), split_axis=0, concat_axis=0, tiled=True)
     got = got.reshape(-1, slice_width + 128)
-    targets = (
-        got[:, slice_width].astype(jnp.int32) * 128 + got[:, slice_width + 1].astype(jnp.int32) - 1
-    )
-    in_sum = scatter_items(got[:, :slice_width], targets, new_count)
     select = select_rows(new_mask, new_count)
     params = jnp.dot(select, table, preferred_element_type=jnp.float32)
     partial_raw = lax.dot_general(
         spread, table, (((1,), (1,)), ((), ())), preferred_element_type=jnp.float32
     ).astype(jnp.bfloat16)
+    partial_raw, got = lax.optimization_barrier((partial_raw, got))
     raw = lax.psum_scatter(partial_raw, "dp", scatter_dimension=0, tiled=True)
-    loss, error = softmax_error(raw.astype(jnp.float32), labels.reshape(-1), vocab_start)
-    piece = lax.all_gather(error, "dp", axis=0, tiled=True)
-    part = jnp.dot(piece, table, preferred_element_type=jnp.float32)
-    d_hidden = finish_hidden(part, groups, shards)
+    loss, piece, summed = error_and_sums(raw, labels.reshape(-1, 1), table, groups, shards)
+    piece = piece.reshape(-1, piece.shape[2])
+    d_hidden = finish_hidden(summed, groups, shards)
+    targets = (
+        got[:, slice_width].astype(jnp.int32) * 128 + got[:, slice_width + 1].astype(jnp.int32) - 1
+    )
+    in_sum = scatter_items(got[:, :slice_width], targets, new_count)
     chosen = lax.dot_general(
         piece, select, (((1,), (1,)), ((), ())), preferred_element_type=jnp.float32
     ).astype(jnp.bfloat16)

time: 262 us -> 216 us (0.82)
  waiting for transfers between devices: 163 us -> 43.2 us
  Pallas kernels: 0 us -> 60.5 us
  blocking collectives: 21.3 us -> 37 us
  matrix products: 28.7 us -> 22.3 us
  local copies, waits for them, and re-layouts: 14.1 us -> 19.3 us
    all_gather x1 -> x0, waiting for transfers between devices: 68.4 us -> none  [body(): piece = lax.all_gather(error, 'dp', axis=0, tiled=True)]
    pallas_call x0 -> x1, Pallas kernels: none -> 60.5 us  [error_and_sums(): pl.pallas_call(functools.partial(error_kernel, groups, shards), out_shape...]
    all_to_all x1, blocking collectives: 11.3 us -> 37 us  [body(): lax.all_to_all(packed, ('dp', 'vocab'), split_axis=0, concat_axis=0, tile...]
    reduce_scatter x1 -> x0, waiting for transfers between devices: 22.8 us -> none  [finish_hidden(): lax.psum_scatter(part.astype(jnp.bfloat16), 'vocab', scatter_dimension=0,...]
    all_gather x1, waiting for transfers between devices: 22 us -> 0.02 us  [gather_states(): lax.all_gather(cut, 'vocab', axis=1, tiled=True)]
    psum x1 -> x0, blocking collectives: 10 us -> none  [softmax_error(): total, picked = lax.psum(jnp.stack([local_total, local_pick]), 'vocab')]
    dot_general x1 -> x0, matrix products: 7.45 us -> none  [body(): part = jnp.dot(piece, table, preferred_element_type=jnp.float32)]
    reduce_scatter x1, waiting for transfers between devices: 48.4 us -> 42.4 us  [body(): raw = lax.psum_scatter(partial_raw, 'dp', scatter_dimension=0, tiled=True)]
  transfers between devices with their start and end apart: 7 -> 5, of which waited for: 5 -> 2; matrix products, arithmetic and copies ran while one was open for 11% -> 11% of each run, Pallas kernels for 0% -> 0%
where the time goes in v2:
time: 216 us; the launch traced here: 215 us
  Pallas kernels  60.5 us (28%)
  waiting for transfers between devices  43.2 us (20%)
  blocking collectives  37 us (17%)
  matrix products  22.3 us (10%)
  local copies, waits for them, and re-layouts  19.3 us (9%)
  starting transfers between devices  14.3 us (7%)
  between operations  14.3 us (7%)
  other arithmetic  4.39 us (2%)
    pallas_call x1, Pallas kernels, error_and_sums(): pl.pallas_call(functools.partial(error_kernel, groups, shards), out_shape...  60.5 us
    reduce_scatter x1, waiting for transfers between devices, body(): raw = lax.psum_scatter(partial_raw, 'dp', scatter_dimension=0, tiled=True)  42.4 us
    all_to_all x1, blocking collectives, body(): lax.all_to_all(packed, ('dp', 'vocab'), split_axis=0, concat_axis=0, tile...  37 us
    ppermute x2, starting transfers between devices, finish_hidden(): got.append(lax.ppermute(piece, ('dp', 'vocab'), pairs))  9.37 us
    unnamed x22, local copies, waits for them, and re-layouts  7.39 us
    dot_general x1, matrix products, body(): lax.dot_general(spread, table, (((1,), (1,)), ((), ())), preferred_elemen...  7.1 us
    dot_general x1, matrix products, body(): params = jnp.dot(select, table, preferred_element_type=jnp.float32)  6.23 us
    dot_general x1, matrix products, body(): lax.dot_general(chosen, spread, (((0,), (0,)), ((), ())), preferred_eleme...  5.76 us
  transfers between devices with their start and end apart: 5, of which 2 were waited for; matrix products, arithmetic and copies ran while one was open for 11% of the time, Pallas kernels for 0%

profile of v2, /device:TPU:6, one launch (start us, length us, event | category | flops | bytes accessed | tf_op | source)
XLA Modules:
  0.0 215.2 jit_solution(8043475011201771959)
XLA Ops:
  7.2 1.2 copy-done
  9.1 4.9 %all-to-all-start = ((bf16[16,4,1152]{2,0,1:T(8,128)(2,1)}), bf16[16,4,1152]{2,0,1:T(8,128)(2,1)S(1)}, u32[]{:S(2)}, u32[]{:S(2)}) async-start(bf16[16,4,1152]{2,0,1:T(8,128)(2,1)} %bitcast.52), calls=%async_computation | async-start | bytes 294912 | tf_op jit(solution)/shard_map/all_to_all | solution.py:230
  14.0 0.8 add_bitcast_fusion.2
  16.7 1.3 convolution_convert_fusion.1
  19.5 0.7 all-to-all-done
  20.2 0.7 copy.57
  21.7 37.0 %all_to_all.21 = bf16[32,12,1280]{2,1,0:T(8,128)(2,1)S(1)} all-to-all(bf16[32,12,1280]{2,1,0:T(8,128)(2,1)S(1)} %copy.63), channel_id=1, replica_groups=mesh['dp'=4,'vocab'=8] {'dp','vocab'}, dimensions={0} | all-to-all | bytes 1966080 | tf_op jit(solution)/shard_map/all_to_all | solution.py:297
  59.0 1.4 copy.58
  60.4 1.0 copy-done.6
  61.4 7.1 %convolution_convert_fusion.2 = bf16[512,2304]{1,0:T(8,128)(2,1)} fusion(bf16[512,1152]{1,0:T(8,128)(2,1)S(1)} %bitcast.57, bf16[2304,1152]{1,0:T(8,128)(2,1)} %table_ref.1), kind=kOutput, calls=%fused_computation.3 | convolution fusion | flops 2719088640 | bytes 8847360 | tf_op jit(solution)/shard_map/dot_general | solution.py:301
  69.6 0.8 reshape.414.label_ref
  71.9 1.5 fusion.15
  73.4 42.4 %reduce-scatter.2.cloned.1.call-done.raw_ref = bf16[128,2304]{1,0:T(8,128)(2,1)} async-done(((bf16[512,2304]{1,0:T(8,128)(2,1)}), bf16[128,2304]{1,0:T(8,128)(2,1)}) %reduce-scatter.2.cloned.1.call-update) | async-done | bytes 589840 | tf_op jit(solution)/shard_map/reduce_scatter | solution.py:305
  115.8 1.1 copy-done.1
  116.9 0.8 copy-done.2
  117.7 60.5 %shard_map.128 = (f32[128,1]{1,0:T(8,128)S(1)}, bf16[4,128,2304]{2,1,0:T(8,128)(2,1)S(1)}, bf16[64,1152]{1,0:T(8,128)(2,1)S(1)}) custom-call(bf16[128,2304]{1,0:T(8,128)(2,1)S(1)} %copy-done.1, s32[128,1]{1,0:T(8,128)S(1)} %copy-done.2, bf16[2304,1152]{1,0:T(8,128)(2,1)} %table_ref.1), custom_call_target="tpu_custom_call" | custom-call | tf_op jit(solution)/shard_map/pallas_call | solution.py:199
  179.5 1.8 reshape.402
  181.3 1.3 constant_dynamic-slice_fusion.1
  183.9 5.0 %collective-permute-start.1 = (bf16[64,576]{1,0:T(8,128)(2,1)}, bf16[64,576]{1,0:T(8,128)(2,1)}, u32[]{:S(2)}, u32[]{:S(2)}) collective-permute-start(bf16[64,576]{1,0:T(8,128)(2,1)} %bitcast.53), channel_id=1, source_target_pairs={{0,1},{1,0},{2,9},{3,8},{4,17},{5,16},{6,25},{7,24},{8,3},{9,2},{1... | collective-permute-start | bytes 221192 | tf_op jit(solution)/shard_map/ppermute | solution.py:248
  188.9 4.4 %collective-permute-start = (bf16[64,576]{1,0:T(8,128)(2,1)}, bf16[64,576]{1,0:T(8,128)(2,1)}, u32[]{:S(2)}, u32[]{:S(2)}) collective-permute-start(bf16[64,576]{1,0:T(8,128)(2,1)} %bitcast.54), channel_id=1, source_target_pairs={{0,0},{1,1},{2,8},{3,9},{4,16},{5,17},{6,24},{7,25},{8,2},{9,3},{1... | collective-permute-start | bytes 221192 | tf_op jit(solution)/shard_map/ppermute | solution.py:248
  193.3 5.8 %multiply_add_fusion = (f32[256,1152]{1,0:T(8,128)}, f32[256,1152]{1,0:T(8,128)}) fusion(f32[256,1152]{1,0:T(8,128)} %param.16, f32[256,1152]{1,0:T(8,128)} %param.17, f32[256,1152]{1,0:T(8,128)} %fusion.15, bf16[512,1152]{1,0:T(8,128)(2,1)} %bitcast.58, bf16[512,2304]{1,0:T(8,128)(2,1)S(1)} %bitcast.56, s32[2304]{0:T(1024)S(1)} %add_bitcast_fusion, ...), kind=kOutput, calls=%fused_computation.13 | convolution fusion | flops 909639680 | bytes 9448704 | tf_op jit(solution)/shard_map/dot_general | solution.py:316
  199.0 6.2 %fusion = f32[256,1152]{1,0:T(8,128)} fusion(bf16[2304,1152]{1,0:T(8,128)(2,1)} %table_ref.1, f32[256,1152]{1,0:T(8,128)} %get-tuple-element.16, f32[256,1152]{1,0:T(8,128)} %get-tuple-element.15, s32[2304]{0:T(1024)S(1)} %add_bitcast_fusion, pred[2304]{0:T(1024)(128)(4,1)S(1)} %broadcast_compare_fusion), kind=kOutput, calls=%fused_computation.6 | convolution fusion | flops 1361903616 | bytes 8858880 | tf_op jit(solution)/shard_map/dot_general | solution.py:300
  206.0 1.0 pad_maximum_fusion
  207.0 1.4 gather_fusion
  (65 shorter events, 10.9 us)
Async XLA Ops:
  7.2 1.3 copy-start
  7.2 10.9 %copy-start.7 = (bf16[1,2,24,4608]{3,2,1,0:T(8,128)(2,1)S(1)}, bf16[1,2,24,4608]{3,2,1,0:T(8,128)(2,1)}, u32[]{:S(2)}) copy-start(bf16[1,2,24,4608]{3,2,1,0:T(8,128)(2,1)} %param.13) | copy-start | bytes 1327108
  9.1 11.1 %all-to-all-start = ((bf16[16,4,1152]{2,0,1:T(8,128)(2,1)}), bf16[16,4,1152]{2,0,1:T(8,128)(2,1)S(1)}, u32[]{:S(2)}, u32[]{:S(2)}) async-start(bf16[16,4,1152]{2,0,1:T(8,128)(2,1)} %bitcast.52), calls=%async_computation | async-start | bytes 294912 | tf_op jit(solution)/shard_map/all_to_all | solution.py:230
  14.0 45.0 %all-gather.2.cloned.1.call-start = ((), (), s32[]{:S(2)}) async-start(), calls=%async_computation.3 | async-start | bytes 1327104 | tf_op jit(solution)/shard_map/all_gather | solution.py:232
  21.0 94.8 %reduce-scatter.2.cloned.1.call-start = ((), (), s32[]{:S(2)}) async-start(), calls=%async_computation.4 | async-start | bytes 2949120 | tf_op jit(solution)/shard_map/reduce_scatter | solution.py:305
  60.4 1.0 copy-start.6
  68.5 0.7 copy-start.8
  68.5 1.1 copy-start.9
  115.8 1.1 copy-start.1
  116.9 0.8 copy-start.2
  178.2 0.7 copy-start.3
  178.9 0.6 copy-start.4
  183.9 22.1 %collective-permute-start.1 = (bf16[64,576]{1,0:T(8,128)(2,1)}, bf16[64,576]{1,0:T(8,128)(2,1)}, u32[]{:S(2)}, u32[]{:S(2)}) collective-permute-start(bf16[64,576]{1,0:T(8,128)(2,1)} %bitcast.53), channel_id=1, source_target_pairs={{0,1},{1,0},{2,9},{3,8},{4,17},{5,16},{6,25},{7,24},{8,3},{9,2},{1... | collective-permute-start | bytes 221192 | tf_op jit(solution)/shard_map/ppermute | solution.py:248
  188.9 17.2 %collective-permute-start = (bf16[64,576]{1,0:T(8,128)(2,1)}, bf16[64,576]{1,0:T(8,128)(2,1)}, u32[]{:S(2)}, u32[]{:S(2)}) collective-permute-start(bf16[64,576]{1,0:T(8,128)(2,1)} %bitcast.54), channel_id=1, source_target_pairs={{0,0},{1,1},{2,8},{3,9},{4,16},{5,17},{6,24},{7,25},{8,2},{9,3},{1... | collective-permute-start | bytes 221192 | tf_op jit(solution)/shard_map/ppermute | solution.py:248
  199.0 6.2 %copy-start.5 = (f32[128,1]{1,0:T(8,128)S(1)}, f32[128,1]{1,0:T(8,128)}, u32[]{:S(2)}) copy-start(f32[128,1]{1,0:T(8,128)} %copy-done.4) | copy-start | bytes 1540
Sparse Core Ops, SparseCore 0:
  21.1 31.9 all-gather.1
  68.7 47.0 reduce-scatter.1

commit v3 on v2

--- a/solution.py
+++ b/solution.py
@@ -32,9 +32,11 @@
     raw_ref,
     label_ref,
     table_ref,
+    packed_ref,
     loss_ref,
     piece_ref,
     sum_ref,
+    got_ref,
     stats,
     square,
     part,
@@ -45,6 +47,8 @@
     line_recv,
     sum_send,
     sum_recv,
+    item_send,
+    item_recv,
 ):
     z = lax.axis_index("dp")
     me = lax.axis_index("vocab")
@@ -93,6 +97,18 @@
 
     for k in range(1, shards):
         stat_copy(k).start()
+
+    def item_copy(k):
+        target = lax.rem(me + k, shards)
+        return pltpu.make_async_remote_copy(
+            src_ref=packed_ref.at[target],
+            dst_ref=got_ref.at[me],
+            send_sem=item_send.at[k],
+            recv_sem=item_recv.at[k],
+            device_id={"vocab": target},
+            device_id_type=MESH,
+        )
+
     gathered = stats[0]
     for k in range(1, shards):
         stat_copy(k).wait_recv()
@@ -106,6 +122,10 @@
     for k in range(1, shards):
         stat_copy(k).wait_send()
 
+    for k in range(1, shards):
+        item_copy(k).start()
+    got_ref[me] = packed_ref[me]
+
     def line_copy(way, s, p, block, target):
         place = piece_ref.at[block, pl.ds(p * half, half)]
         return pltpu.make_async_remote_copy(
@@ -180,6 +200,8 @@
         ).wait()
         summed = summed + inbox[source].astype(jnp.float32)
     sum_ref[...] = summed.astype(jnp.bfloat16)
+    for k in range(1, shards):
+        item_copy(k).wait()
     for s in range(groups - 1):
         for p in range(halves):
             for way in range(2):
@@ -191,7 +213,7 @@
                     line_copy(way, s, p, block, target).wait_send()
 
 
-def error_and_sums(raw, labels, table, groups, shards):
+def error_and_sums(raw, labels, table, packed, groups, shards):
     tokens, rows_here = raw.shape
     slice_width = table.shape[1]
     chunk_rows = groups * tokens // shards
@@ -202,9 +224,10 @@
             jax.ShapeDtypeStruct((tokens, 1), jnp.float32),
             jax.ShapeDtypeStruct((groups, tokens, rows_here), jnp.bfloat16),
             jax.ShapeDtypeStruct((chunk_rows, slice_width), jnp.bfloat16),
-        ),
-        in_specs=[vmem] * 3,
-        out_specs=(vmem,) * 3,
+            jax.ShapeDtypeStruct(packed.shape, packed.dtype),
+        ),
+        in_specs=[vmem] * 4,
+        out_specs=(vmem,) * 4,
         scratch_shapes=[
             pltpu.VMEM((shards, 8, tokens), jnp.float32),
             pltpu.VMEM((128, tokens), jnp.float32),
@@ -216,20 +239,122 @@
             pltpu.SemaphoreType.DMA((2, groups, 2)),
             pltpu.SemaphoreType.DMA((shards,)),
             pltpu.SemaphoreType.DMA((shards,)),
+            pltpu.SemaphoreType.DMA((shards,)),
+            pltpu.SemaphoreType.DMA((shards,)),
         ],
         compiler_params=pltpu.CompilerParams(
             collective_id=0, has_side_effects=True, vmem_limit_bytes=48 * 1024 * 1024
         ),
-    )(raw, labels, table)
-
-
-def gather_states(states, shards):
+    )(raw, labels, table, packed)
+
+
+def spread_kernel(
+    groups,
+    shards,
+    mine_ref,
+    items_ref,
+    out_ref,
+    got_ref,
+    cut_send,
+    cut_recv,
+    item_send,
+    item_recv,
+    plane_send,
+    plane_recv,
+):
+    z = lax.axis_index("dp")
+    me = lax.axis_index("vocab")
+    barrier = pltpu.get_barrier_semaphore()
+    for k in range(1, shards):
+        pl.semaphore_signal(
+            barrier, inc=1, device_id={"vocab": lax.rem(me + k, shards)}, device_id_type=MESH
+        )
+    for j in range(1, groups):
+        pl.semaphore_signal(
+            barrier, inc=1, device_id={"dp": lax.rem(z + j, groups)}, device_id_type=MESH
+        )
+    pl.semaphore_wait(barrier, shards + groups - 2)
+
+    def cut_copy(j):
+        target = lax.rem(z + j, groups)
+        return pltpu.make_async_remote_copy(
+            src_ref=mine_ref.at[target],
+            dst_ref=out_ref.at[me, z],
+            send_sem=cut_send.at[j],
+            recv_sem=cut_recv.at[j],
+            device_id={"dp": target},
+            device_id_type=MESH,
+        )
+
+    def item_copy(j):
+        target = lax.rem(z + j, groups)
+        return pltpu.make_async_remote_copy(
+            src_ref=items_ref.at[target],
+            dst_ref=got_ref.at[z],
+            send_sem=item_send.at[j],
+            recv_sem=item_recv.at[j],
+            device_id={"dp": target},
+            device_id_type=MESH,
+        )
+
+    def plane_copy(j, k):
+        place = out_ref.at[me, lax.rem(z + groups - j, groups)]
+        return pltpu.make_async_remote_copy(
+            src_ref=place,
+            dst_ref=place,
+            send_sem=plane_send.at[j, k],
+            recv_sem=plane_recv.at[j, k],
+            device_id={"vocab": lax.rem(me + k, shards)},
+            device_id_type=MESH,
+        )
+
+    for j in range(1, groups):
+        cut_copy(j).start()
+    for j in range(1, groups):
+        item_copy(j).start()
+    out_ref[me, z] = mine_ref[z]
+    got_ref[z] = items_ref[z]
+    for j in range(groups):
+        if j > 0:
+            cut_copy(j).wait_recv()
+        for k in range(1, shards):
+            plane_copy(j, k).start()
+    for j in range(groups):
+        for k in range(1, shards):
+            plane_copy(j, k).wait()
+    for j in range(1, groups):
+        cut_copy(j).wait_send()
+        item_copy(j).wait()
+
+
+def spread_states(states, items, groups, shards):
     share = states.shape[0] // shards
     mine = lax.dynamic_slice_in_dim(states, lax.axis_index("vocab") * share, share, 0)
-    groups = lax.axis_size("dp")
-    cut = lax.all_to_all(mine, "dp", split_axis=1, concat_axis=0, tiled=True)
-    cut = cut.reshape(groups, share, -1)
-    return lax.all_gather(cut, "vocab", axis=1, tiled=True).reshape(groups * share * shards, -1)
+    mine = mine.reshape(share, groups, -1).transpose(1, 0, 2)
+    vmem = pl.BlockSpec(memory_space=pltpu.VMEM)
+    dma = pltpu.SemaphoreType.DMA
+    spread, got = pl.pallas_call(
+        functools.partial(spread_kernel, groups, shards),
+        out_shape=(
+            jax.ShapeDtypeStruct((shards,) + mine.shape, mine.dtype),
+            jax.ShapeDtypeStruct(items.shape, items.dtype),
+        ),
+        in_specs=[vmem] * 2,
+        out_specs=(vmem,) * 2,
+        scratch_shapes=[
+            dma((groups,)),
+            dma((groups,)),
+            dma((groups,)),
+            dma((groups,)),
+            dma((groups, shards)),
+            dma((groups, shards)),
+        ],
+        compiler_params=pltpu.CompilerParams(
+            collective_id=1, has_side_effects=True, vmem_limit_bytes=24 * 1024 * 1024
+        ),
+    )(mine, items)
+    spread = spread.transpose(1, 0, 2, 3).reshape(groups * share * shards, -1)
+    return spread, got.reshape(-1, items.shape[2])
 
 
 def finish_hidden(mine, groups, shards):
@@ -250,21 +375,22 @@
     return jnp.stack(got)[order].reshape(ratio * rows, columns // ratio)
 
 
-def pack_items(rows, owner, slot, shards, capacity, groups):
+def code_items(rows, owner, slot, groups):
+    mark = slot + 1
+    code = jnp.stack([owner, mark // 128, mark % 128], axis=1).astype(jnp.bfloat16)
+    code = jnp.broadcast_to(jnp.pad(code, ((0, 0), (0, 125))), (groups, rows.shape[0], 128))
+    cut = rows.reshape(rows.shape[0], groups, -1).transpose(1, 0, 2)
+    return jnp.concatenate([cut, code], axis=2)
+
+
+def pack_items(items, slice_width, shards, capacity):
+    owner = items[:, slice_width].astype(jnp.int32)
     onehot = (owner[:, None] == jnp.arange(shards, dtype=jnp.int32)[None, :]).astype(jnp.int32)
-    running = jnp.cumsum(onehot, axis=0)
-    ranked = jnp.sum(onehot * running, axis=1) - 1
+    ranked = jnp.sum(onehot * jnp.cumsum(onehot, axis=0), axis=1) - 1
     place = owner * capacity + ranked
     placing = jnp.arange(shards * capacity, dtype=jnp.int32)[:, None] == place[None, :]
-    sent = jnp.dot(placing.astype(jnp.bfloat16), rows, preferred_element_type=jnp.float32).astype(
-        jnp.bfloat16
-    )
-    targets = jnp.sum(placing.astype(jnp.int32) * (slot + 1)[None, :], axis=1)
-    sent = sent.reshape(shards, capacity, groups, -1).transpose(2, 0, 1, 3)
-    high, low = (targets // 128).astype(jnp.bfloat16), (targets % 128).astype(jnp.bfloat16)
-    code = jnp.stack([high, low], axis=1).reshape(1, shards, capacity, 2)
-    code = jnp.broadcast_to(jnp.pad(code, ((0, 0), (0, 0), (0, 0), (0, 126))), (groups, shards, capacity, 128))
-    return jnp.concatenate([sent, code], axis=3)
+    packed = jnp.dot(placing.astype(jnp.bfloat16), items, preferred_element_type=jnp.float32)
+    return packed.astype(jnp.bfloat16).reshape(shards, capacity, -1)
 
 
 def scatter_items(rows, targets, new_count):
@@ -284,30 +410,31 @@
     groups = lax.axis_size("dp")
     items_here = in_grad.shape[2]
     capacity = max(2, (2 * items_here + shards - 1) // shards)
-    spread = gather_states(hidden.reshape(blocks * span, width), shards)
-    packed = jnp.concatenate(
-        [
-            pack_items(
-                in_grad[0, c], item_owner[0, c, :, 0], item_slot[0, c], shards, capacity, groups
-            )
-            for c in range(blocks)
-        ],
-        axis=2,
-    ).reshape(groups * shards, blocks * capacity, slice_width + 128)
-    got = lax.all_to_all(packed, ("dp", "vocab"), split_axis=0, concat_axis=0, tiled=True)
-    got = got.reshape(-1, slice_width + 128)
+    coded = code_items(
+        in_grad.reshape(blocks * items_here, width),
+        item_owner.reshape(-1),
+        item_slot.reshape(-1),
+        groups,
+    )
+    spread, items = spread_states(hidden.reshape(blocks * span, width), coded, groups, shards)
+    packed = pack_items(items, slice_width, shards, groups * blocks * capacity)
     select = select_rows(new_mask, new_count)
     params = jnp.dot(select, table, preferred_element_type=jnp.float32)
     partial_raw = lax.dot_general(
         spread, table, (((1,), (1,)), ((), ())), preferred_element_type=jnp.float32
     ).astype(jnp.bfloat16)
-    partial_raw, got = lax.optimization_barrier((partial_raw, got))
     raw = lax.psum_scatter(partial_raw, "dp", scatter_dimension=0, tiled=True)
-    loss, piece, summed = error_and_sums(raw, labels.reshape(-1, 1), table, groups, shards)
+    raw, packed, params = lax.optimization_barrier((raw, packed, params))
+    loss, piece, summed, got = error_and_sums(
+        raw, labels.reshape(-1, 1), table, packed, groups, shards
+    )
+    got = got.reshape(-1, got.shape[2])
     piece = piece.reshape(-1, piece.shape[2])
     d_hidden = finish_hidden(summed, groups, shards)
     targets = (
-        got[:, slice_width].astype(jnp.int32) * 128 + got[:, slice_width + 1].astype(jnp.int32) - 1
+        got[:, slice_width + 1].astype(jnp.int32) * 128
+        + got[:, slice_width + 2].astype(jnp.int32)
+        - 1
     )
     in_sum = scatter_items(got[:, :slice_width], targets, new_count)
     chosen = lax.dot_general(

time: 216 us -> 178 us (0.82)
  blocking collectives: 37 us -> 0 us
  Pallas kernels: 60.5 us -> 79.3 us
  local copies, waits for them, and re-layouts: 19.3 us -> 9.14 us
  starting transfers between devices: 14.3 us -> 9.5 us
  waiting for transfers between devices: 43.2 us -> 40.3 us
    all_to_all x1 -> x0, blocking collectives: 37 us -> none  [body(): lax.all_to_all(packed, ('dp', 'vocab'), split_axis=0, concat_axis=0, tile...]
    pallas_call x0 -> x1, Pallas kernels: none -> 18.6 us  [spread_states(): pl.pallas_call(functools.partial(spread_kernel, groups, shards), out_shap...]
    all_to_all x1 -> x0, starting transfers between devices: 4.87 us -> none  [gather_states(): cut = lax.all_to_all(mine, 'dp', split_axis=1, concat_axis=0, tiled=True)]
    unnamed x22 -> x16, local copies, waits for them, and re-layouts: 7.39 us -> 3.56 us
    reduce_scatter x1, waiting for transfers between devices: 42.4 us -> 40.3 us  [body(): raw = lax.psum_scatter(partial_raw, 'dp', scatter_dimension=0, tiled=True)]
  transfers between devices with their start and end apart: 5 -> 3, of which waited for: 2 -> 1; matrix products, arithmetic and copies ran while one was open for 11% -> 10% of each run, Pallas kernels for 0% -> 0%
where the time goes in v3:
time: 178 us
  Pallas kernels  79.3 us (45%)
  waiting for transfers between devices  40.3 us (23%)
  matrix products  22.4 us (13%)
  between operations  14.3 us (8%)
  starting transfers between devices  9.5 us (5%)
  local copies, waits for them, and re-layouts  9.14 us (5%)
  other arithmetic  2.89 us (2%)
    pallas_call x1, Pallas kernels, error_and_sums(): pl.pallas_call(functools.partial(error_kernel, groups, shards), out_shape...  60.7 us
    reduce_scatter x1, waiting for transfers between devices, body(): raw = lax.psum_scatter(partial_raw, 'dp', scatter_dimension=0, tiled=True)  40.3 us
    pallas_call x1, Pallas kernels, spread_states(): pl.pallas_call(functools.partial(spread_kernel, groups, shards), out_shap...  18.6 us
    ppermute x2, starting transfers between devices, finish_hidden(): got.append(lax.ppermute(piece, ('dp', 'vocab'), pairs))  9.46 us
    dot_general x1, matrix products, body(): lax.dot_general(chosen, spread, (((0,), (0,)), ((), ())), preferred_eleme...  7.68 us
    dot_general x1, matrix products, body(): lax.dot_general(spread, table, (((1,), (1,)), ((), ())), preferred_elemen...  7.54 us
    dot_general x1, matrix products, body(): params = jnp.dot(select, table, preferred_element_type=jnp.float32)  5.34 us
  transfers between devices with their start and end apart: 3, of which 1 were waited for; matrix products, arithmetic and copies ran while one was open for 10% of the time, Pallas kernels for 0%

profile of v3, /device:TPU:6, one launch (start us, length us, event | category | flops | bytes accessed | tf_op | source)
XLA Modules:
  0.0 177.9 jit_solution(2674687178372724439)
XLA Ops:
  7.2 0.8 convert_reduce_fusion
  8.1 0.7 broadcast_add_fusion
  9.1 1.1 reshape_reshape.6
  10.3 18.6 %shard_map.128 = (bf16[8,4,16,1152]{3,2,1,0:T(8,128)(2,1)S(1)}, bf16[4,48,1280]{2,1,0:T(8,128)(2,1)S(1)}) custom-call(bf16[4,16,1152]{2,1,0:T(8,128)(2,1)S(1)} %bitcast.54, bf16[4,48,1280]{2,1,0:T(8,128)(2,1)S(1)} %pad_maximum_fusion.items_ref), custom_call_target="tpu_custom_call" | custom-call | tf_op jit(solution)/shard_map/pallas_call | solution.py:336
  28.9 1.1 copy.19
  30.0 7.5 %convolution_convert_fusion = bf16[512,2304]{1,0:T(8,128)(2,1)} fusion(bf16[512,1152]{1,0:T(8,128)(2,1)} %bitcast.4, bf16[2304,1152]{1,0:T(8,128)(2,1)} %table_ref.1), kind=kOutput, calls=%fused_computation.1 | convolution fusion | flops 2719088640 | bytes 8847360 | tf_op jit(solution)/shard_map/dot_general | solution.py:423
  37.6 0.7 copy-done.3
  38.3 0.3 reduce-window.19
  39.0 0.6 reduce-window.15
  39.6 0.2 slice_reduce_fusion.1
  40.2 0.4 convolution_convert_fusion.1
  40.6 5.3 %fusion.3 = f32[256,1152]{1,0:T(8,128)} fusion(bf16[2304,1152]{1,0:T(8,128)(2,1)} %table_ref.1, s32[2304]{0:T(1024)S(1)} %add_bitcast_fusion, pred[2304]{0:T(1024)(128)(4,1)S(1)} %broadcast_compare_fusion), kind=kOutput, calls=%fused_computation.7 | convolution fusion | flops 1360134144 | bytes 6499584 | tf_op jit(solution)/shard_map/dot_general | solution.py:422
  45.9 40.3 %reduce-scatter.2.cloned.1.call-done.raw_ref = bf16[128,2304]{1,0:T(8,128)(2,1)} async-done(((bf16[512,2304]{1,0:T(8,128)(2,1)}), bf16[128,2304]{1,0:T(8,128)(2,1)}) %reduce-scatter.2.cloned.1.call-update) | async-done | bytes 589840 | tf_op jit(solution)/shard_map/reduce_scatter | solution.py:426
  86.2 1.1 copy-done.1
  87.3 60.7 %shard_map.129 = (f32[128,1]{1,0:T(8,128)S(1)}, bf16[4,128,2304]{2,1,0:T(8,128)(2,1)S(1)}, bf16[64,1152]{1,0:T(8,128)(2,1)S(1)}, bf16[8,48,1280]{2,1,0:T(8,128)(2,1)S(1)}) custom-call(bf16[128,2304]{1,0:T(8,128)(2,1)S(1)} %copy-done.1, s32[128,1]{1,0:T(8,128)S(1)} %reshape.258.label_ref, bf16[2304,1152]{1,0:T(8,128)(2,1)} %table_ref.1, ...), custom_call_target="tpu_custom_call" | custom-call | tf_op jit(solution)/shard_map/pallas_call | solution.py:221
  148.0 1.4 copy-done.2
  149.4 0.2 reshape.245
  149.6 0.3 constant_dynamic-slice_fusion.1
  150.0 5.0 %collective-permute-start.1 = (bf16[64,576]{1,0:T(8,128)(2,1)S(1)}, bf16[64,576]{1,0:T(8,128)(2,1)S(1)}, u32[]{:S(2)}, u32[]{:S(2)}) collective-permute-start(bf16[64,576]{1,0:T(8,128)(2,1)S(1)} %bitcast.62), channel_id=1, source_target_pairs={{0,1},{1,0},{2,9},{3,8},{4,17},{5,16},{6,25},{7,24},{8,3},{9,2},{1... | collective-permute-start | bytes 221192 | tf_op jit(solution)/shard_map/ppermute | solution.py:373
  155.0 4.4 %collective-permute-start = (bf16[64,576]{1,0:T(8,128)(2,1)S(1)}, bf16[64,576]{1,0:T(8,128)(2,1)S(1)}, u32[]{:S(2)}, u32[]{:S(2)}) collective-permute-start(bf16[64,576]{1,0:T(8,128)(2,1)S(1)} %bitcast.61), channel_id=1, source_target_pairs={{0,0},{1,1},{2,8},{3,9},{4,16},{5,17},{6,24},{7,25},{8,2},{9,3},{1... | collective-permute-start | bytes 221192 | tf_op jit(solution)/shard_map/ppermute | solution.py:373
  159.8 1.5 fusion.15
  161.3 7.7 %multiply_add_fusion = (f32[256,1152]{1,0:T(8,128)}, f32[256,1152]{1,0:T(8,128)}, f32[256,1152]{1,0:T(8,128)}) fusion(f32[256,1152]{1,0:T(8,128)} %fusion.3, f32[256,1152]{1,0:T(8,128)} %param.16, f32[256,1152]{1,0:T(8,128)} %param.17, f32[256,1152]{1,0:T(8,128)} %fusion.15, bf16[512,1152]{1,0:T(8,128)(2,1)} %bitcast.4, bf16[512,2304]{1,0:T(8,128)(2,1)} %bitcast.55, ...), kind=kOutput, calls=%fused_computation.11 | convolution fusion | flops 911409152 | bytes 11808000 | tf_op jit(solution)/shard_map/dot_general | solution.py:443
  169.1 0.7 reshape.244
  169.8 1.2 gather_fusion
  (49 shorter events, 1.8 us)
Async XLA Ops:
  7.2 1.8 %copy-start = (bf16[1,2,64,4608]{3,2,1,0:T(8,128)(2,1)S(1)}, bf16[1,2,64,4608]{3,2,1,0:T(8,128)(2,1)}, u32[]{:S(2)}) copy-start(bf16[1,2,64,4608]{3,2,1,0:T(8,128)(2,1)} %param.9) | copy-start | bytes 3538948
  7.2 79.0 %reduce-scatter.2.cloned.1.call-start = ((), (), s32[]{:S(2)}) async-start(), calls=%async_computation.1 | async-start | bytes 2949120 | tf_op jit(solution)/shard_map/reduce_scatter | solution.py:426
  37.6 0.7 copy-start.3
  37.6 1.1 copy-start.4
  86.2 1.1 copy-start.1
  148.0 1.4 copy-start.2
  150.0 19.8 %collective-permute-start.1 = (bf16[64,576]{1,0:T(8,128)(2,1)S(1)}, bf16[64,576]{1,0:T(8,128)(2,1)S(1)}, u32[]{:S(2)}, u32[]{:S(2)}) collective-permute-start(bf16[64,576]{1,0:T(8,128)(2,1)S(1)} %bitcast.62), channel_id=1, source_target_pairs={{0,1},{1,0},{2,9},{3,8},{4,17},{5,16},{6,25},{7,24},{8,3},{9,2},{1... | collective-permute-start | bytes 221192 | tf_op jit(solution)/shard_map/ppermute | solution.py:373
  155.0 14.7 %collective-permute-start = (bf16[64,576]{1,0:T(8,128)(2,1)S(1)}, bf16[64,576]{1,0:T(8,128)(2,1)S(1)}, u32[]{:S(2)}, u32[]{:S(2)}) collective-permute-start(bf16[64,576]{1,0:T(8,128)(2,1)S(1)} %bitcast.61), channel_id=1, source_target_pairs={{0,0},{1,1},{2,8},{3,9},{4,16},{5,17},{6,24},{7,25},{8,2},{9,3},{1... | collective-permute-start | bytes 221192 | tf_op jit(solution)/shard_map/ppermute | solution.py:373
Sparse Core Ops, SparseCore 0:
  37.7 48.4 reduce-scatter.1

commit v4 on v3

--- a/solution.py
+++ b/solution.py
@@ -29,10 +29,12 @@
 def error_kernel(
     groups,
     shards,
-    raw_ref,
+    spread_ref,
     label_ref,
     table_ref,
     packed_ref,
+    select_ref,
+    params_ref,
     loss_ref,
     piece_ref,
     sum_ref,
@@ -49,10 +51,16 @@
     sum_recv,
     item_send,
     item_recv,
+    outbox,
+    logits_in,
+    raw,
+    chain_send,
+    chain_recv,
 ):
     z = lax.axis_index("dp")
     me = lax.axis_index("vocab")
-    tokens, rows_here = raw_ref.shape
+    tokens = spread_ref.shape[1]
+    rows_here = table_ref.shape[0]
     chunk_rows = sum_ref.shape[0]
     ratio = shards // groups
     halves = 2
@@ -72,7 +80,74 @@
     def _():
         pl.semaphore_signal(barrier, inc=1, device_id={"dp": z - 1}, device_id_type=MESH)
 
-    capped = cap_value * jnp.tanh(raw_ref[...].astype(jnp.float32) / cap_value)
+    near = (z < groups - 1).astype(jnp.int32) + (z > 0).astype(jnp.int32)
+    pl.semaphore_wait(barrier, shards - 1 + near)
+
+    def partial_logits(block):
+        return lax.dot_general(
+            spread_ref[block],
+            table_ref[...],
+            (((1,), (1,)), ((), ())),
+            preferred_element_type=jnp.float32,
+        )
+
+    def chain_copy(way, s):
+        return pltpu.make_async_remote_copy(
+            src_ref=outbox.at[way, s],
+            dst_ref=logits_in.at[way, s],
+            send_sem=chain_send.at[way, s],
+            recv_sem=chain_recv.at[way, s],
+            device_id={"dp": z + 1 - 2 * way},
+            device_id_type=MESH,
+        )
+
+    for s in range(groups - 1):
+
+        @pl.loop(0, 2)
+        def _(i, s=s):
+            way = lax.rem(i + (2 * z) // groups, 2)
+            block = groups - 1 - s + way * (2 * s - groups + 1)
+
+            @pl.when((block - z) * (1 - 2 * way) > 0)
+            def _():
+                raw[...] = partial_logits(block)
+
+                @pl.when(z * (1 - way) + (groups - 1 - z) * way > 0)
+                def _():
+                    chain_copy(way, s).wait_recv()
+                    raw[...] += logits_in[way, s].astype(jnp.float32)
+
+                outbox[way, s] = raw[...].astype(jnp.bfloat16)
+                chain_copy(way, s).start()
+
+        if s == 0:
+            params_ref[...] = jnp.dot(
+                select_ref[...], table_ref[...], preferred_element_type=jnp.float32
+            )
+
+    raw[...] = partial_logits(z)
+
+    @pl.when(z > 0)
+    def _():
+        chain_copy(0, groups - 1 - z).wait_recv()
+        raw[...] += logits_in[0, groups - 1 - z].astype(jnp.float32)
+
+    @pl.when(z < groups - 1)
+    def _():
+        chain_copy(1, z).wait_recv()
+        raw[...] += logits_in[1, z].astype(jnp.float32)
+
+    for s in range(groups - 1):
+
+        @pl.loop(0, 2)
+        def _(way, s=s):
+            block = groups - 1 - s + way * (2 * s - groups + 1)
+
+            @pl.when((block - z) * (1 - 2 * way) > 0)
+            def _():
+                chain_copy(way, s).wait_send()
+
+    capped = cap_value * jnp.tanh(raw[...] / cap_value)
     expd = jnp.exp(capped)
     ids = lax.broadcasted_iota(jnp.int32, (tokens, rows_here), 1) + me * rows_here
     hits = ids == label_ref[...]
@@ -82,9 +157,6 @@
     square[...] = jnp.where(lane == 0, local_total, jnp.where(lane == 1, local_pick, 0.0)).T
     stats[0] = square[0:8, :]
 
-    near = (z < groups - 1).astype(jnp.int32) + (z > 0).astype(jnp.int32)
-    pl.semaphore_wait(barrier, shards - 1 + near)
-
     def stat_copy(k):
         return pltpu.make_async_remote_copy(
             src_ref=stats.at[0],
@@ -213,21 +285,22 @@
                     line_copy(way, s, p, block, target).wait_send()
 
 
-def error_and_sums(raw, labels, table, packed, groups, shards):
-    tokens, rows_here = raw.shape
+def error_and_sums(spread, labels, table, packed, select, groups, shards):
+    tokens, rows_here = spread.shape[1], table.shape[0]
     slice_width = table.shape[1]
     chunk_rows = groups * tokens // shards
     vmem = pl.BlockSpec(memory_space=pltpu.VMEM)
     return pl.pallas_call(
         functools.partial(error_kernel, groups, shards),
         out_shape=(
+            jax.ShapeDtypeStruct((select.shape[0], slice_width), jnp.float32),
             jax.ShapeDtypeStruct((tokens, 1), jnp.float32),
             jax.ShapeDtypeStruct((groups, tokens, rows_here), jnp.bfloat16),
             jax.ShapeDtypeStruct((chunk_rows, slice_width), jnp.bfloat16),
             jax.ShapeDtypeStruct(packed.shape, packed.dtype),
         ),
-        in_specs=[vmem] * 4,
-        out_specs=(vmem,) * 4,
+        in_specs=[vmem] * 5,
+        out_specs=(vmem,) * 5,
         scratch_shapes=[
             pltpu.VMEM((shards, 8, tokens), jnp.float32),
             pltpu.VMEM((128, tokens), jnp.float32),
@@ -241,11 +314,16 @@
             pltpu.SemaphoreType.DMA((shards,)),
             pltpu.SemaphoreType.DMA((shards,)),
             pltpu.SemaphoreType.DMA((shards,)),
+            pltpu.VMEM((2, groups - 1, tokens, rows_here), jnp.bfloat16),
+            pltpu.VMEM((2, groups - 1, tokens, rows_here), jnp.bfloat16),
+            pltpu.VMEM((tokens, rows_here), jnp.float32),
+            pltpu.SemaphoreType.DMA((2, groups)),
+            pltpu.SemaphoreType.DMA((2, groups)),
         ],
         compiler_params=pltpu.CompilerParams(
-            collective_id=0, has_side_effects=True, vmem_limit_bytes=48 * 1024 * 1024
+            collective_id=0, has_side_effects=True, vmem_limit_bytes=58 * 1024 * 1024
         ),
-    )(raw, labels, table, packed)
+    )(spread, labels, table, packed, select)
 
 
 def spread_kernel(
@@ -419,14 +497,14 @@
     spread, items = spread_states(hidden.reshape(blocks * span, width), coded, groups, shards)
     packed = pack_items(items, slice_width, shards, groups * blocks * capacity)
     select = select_rows(new_mask, new_count)
-    params = jnp.dot(select, table, preferred_element_type=jnp.float32)
-    partial_raw = lax.dot_general(
-        spread, table, (((1,), (1,)), ((), ())), preferred_element_type=jnp.float32
-    ).astype(jnp.bfloat16)
-    raw = lax.psum_scatter(partial_raw, "dp", scatter_dimension=0, tiled=True)
-    raw, packed, params = lax.optimization_barrier((raw, packed, params))
-    loss, piece, summed, got = error_and_sums(
-        raw, labels.reshape(-1, 1), table, packed, groups, shards
+    params, loss, piece, summed, got = error_and_sums(
+        spread.reshape(groups, blocks * span, slice_width),
+        labels.reshape(-1, 1),
+        table,
+        packed,
+        select,
+        groups,
+        shards,
     )
     got = got.reshape(-1, got.shape[2])
     piece = piece.reshape(-1, piece.shape[2])

time: 178 us -> 168 us (0.944)
  Pallas kernels: 79.3 us -> 130 us
  waiting for transfers between devices: 40.3 us -> 0.01 us
  between operations: 14.3 us -> 0.9 us
  matrix products: 22.4 us -> 10.2 us
  other arithmetic: 2.89 us -> 6.47 us
    pallas_call x1, Pallas kernels: 60.7 us -> 112 us  [error_and_sums(): pl.pallas_call(functools.partial(error_kernel, groups, shards), out_shape...]
    reduce_scatter x1 -> x0, waiting for transfers between devices: 40.3 us -> none  [body(): raw = lax.psum_scatter(partial_raw, 'dp', scatter_dimension=0, tiled=True)]
    dot_general x2 -> x0, matrix products: 12.9 us -> none  [the longest x1 7.54 us: body(): lax.dot_general(spread, table, (((1,), (1,)), ((), ())), preferred_elemen...]
  transfers between devices with their start and end apart: 3 -> 2, of which waited for: 1 -> 0; matrix products, arithmetic and copies ran while one was open for 10% -> 7% of each run, Pallas kernels for 0% -> 0%
where the time goes in v4:
time: 168 us; the launch traced here: 167 us
  Pallas kernels  130 us (77%)
  matrix products  10.2 us (6%)
  starting transfers between devices  9.96 us (6%)
  local copies, waits for them, and re-layouts  9.48 us (6%)
  other arithmetic  6.47 us (4%)
    pallas_call x1, Pallas kernels, error_and_sums(): pl.pallas_call(functools.partial(error_kernel, groups, shards), out_shape...  112 us
    pallas_call x1, Pallas kernels, spread_states(): pl.pallas_call(functools.partial(spread_kernel, groups, shards), out_shap...  18.6 us
    ppermute x2, starting transfers between devices, finish_hidden(): got.append(lax.ppermute(piece, ('dp', 'vocab'), pairs))  9.96 us
    dot_general x1, matrix products, body(): lax.dot_general(chosen, spread, (((0,), (0,)), ((), ())), preferred_eleme...  7.35 us
  transfers between devices with their start and end apart: 2, of which 0 were waited for; matrix products, arithmetic and copies ran while one was open for 7% of the time, Pallas kernels for 0%

profile of v4, /device:TPU:6, one launch (start us, length us, event | category | flops | bytes accessed | tf_op | source)
XLA Modules:
  0.0 167.5 jit_solution(8649082694202439815)
XLA Ops:
  0.7 0.8 convert_reduce_fusion
  1.5 0.7 broadcast_add_fusion
  2.5 1.1 reshape_reshape.9
  3.8 18.6 %shard_map.128 = (bf16[8,4,16,1152]{3,2,1,0:T(8,128)(2,1)S(1)}, bf16[4,48,1280]{2,1,0:T(8,128)(2,1)S(1)}) custom-call(bf16[4,16,1152]{2,1,0:T(8,128)(2,1)S(1)} %bitcast.49, bf16[4,48,1280]{2,1,0:T(8,128)(2,1)S(1)} %pad_maximum_fusion.items_ref), custom_call_target="tpu_custom_call" | custom-call | tf_op jit(solution)/shard_map/pallas_call | solution.py:414
  23.1 0.8 reshape.258.label_ref
  23.9 1.1 copy.20
  25.0 0.6 reduce-window.15
  26.0 1.4 convolution_convert_fusion
  27.4 1.4 fusion.3.select_ref
  28.7 111.8 %shard_map.129 = (f32[256,1152]{1,0:T(8,128)}, f32[128,1]{1,0:T(8,128)}, bf16[4,128,2304]{2,1,0:T(8,128)(2,1)}, bf16[64,1152]{1,0:T(8,128)(2,1)}, bf16[8,48,1280]{2,1,0:T(8,128)(2,1)}) custom-call(bf16[4,128,1152]{2,1,0:T(8,128)(2,1)} %bitcast.50, s32[128,1]{1,0:T(8,128)} %reshape.258.label_ref, bf16[2304,1152]{1,0:T(8,128)(2,1)} %table_ref.1, ...), custom_call_target="tpu_custom_call" | custom-call | tf_op jit(solution)/shard_map/pallas_call | solution.py:293
  140.6 1.2 reshape.244
  141.8 0.3 constant_dynamic-slice_fusion.1
  142.2 0.6 copy.41
  142.8 5.5 %collective-permute-start.1 = (bf16[64,576]{1,0:T(8,128)(2,1)}, bf16[64,576]{1,0:T(8,128)(2,1)}, u32[]{:S(2)}, u32[]{:S(2)}) collective-permute-start(bf16[64,576]{1,0:T(8,128)(2,1)} %bitcast.43), channel_id=1, source_target_pairs={{0,1},{1,0},{2,9},{3,8},{4,17},{5,16},{6,25},{7,24},{8,3},{9,2},{1... | collective-permute-start | bytes 221192 | tf_op jit(solution)/shard_map/ppermute | solution.py:451
  148.3 0.6 copy.42
  149.0 4.5 %collective-permute-start = (bf16[64,576]{1,0:T(8,128)(2,1)}, bf16[64,576]{1,0:T(8,128)(2,1)}, u32[]{:S(2)}, u32[]{:S(2)}) collective-permute-start(bf16[64,576]{1,0:T(8,128)(2,1)} %bitcast.44), channel_id=1, source_target_pairs={{0,0},{1,1},{2,8},{3,9},{4,16},{5,17},{6,24},{7,25},{8,2},{9,3},{1... | collective-permute-start | bytes 221192 | tf_op jit(solution)/shard_map/ppermute | solution.py:451
  153.4 0.6 fusion.19
  154.1 0.7 reshape.243
  154.9 0.7 copy.31
  155.7 0.7 add_reduce_fusion
  156.4 1.5 fusion.12
  157.9 7.3 %multiply_add_fusion = (f32[256,1152]{1,0:T(8,128)}, f32[256,1152]{1,0:T(8,128)}, f32[256,1152]{1,0:T(8,128)}) fusion(f32[256,1152]{1,0:T(8,128)} %get-tuple-element.18, f32[256,1152]{1,0:T(8,128)} %param.16, f32[256,1152]{1,0:T(8,128)} %param.17, f32[256,1152]{1,0:T(8,128)} %fusion.12, bf16[512,1152]{1,0:T(8,128)(2,1)S(1)} %bitcast.51, ...), kind=kOutput, calls=%fused_computation.10 | convolution fusion | flops 911409152 | bytes 11808000 | tf_op jit(solution)/shard_map/dot_general | solution.py:521
  165.3 1.0 pad_maximum_fusion.1
  166.2 1.2 gather_fusion
  (49 shorter events, 1.9 us)
Async XLA Ops:
  0.6 1.8 %copy-start = (bf16[1,2,64,4608]{3,2,1,0:T(8,128)(2,1)S(1)}, bf16[1,2,64,4608]{3,2,1,0:T(8,128)(2,1)}, u32[]{:S(2)}) copy-start(bf16[1,2,64,4608]{3,2,1,0:T(8,128)(2,1)} %param.9) | copy-start | bytes 3538948
  3.6 18.9 %copy-start.4 = (s32[2304]{0:T(1024)S(1)}, s32[2304]{0:T(1024)}, u32[]{:S(2)}) copy-start(s32[2304]{0:T(1024)} %param.11) | copy-start | bytes 27652
  3.7 19.4 %copy-start.5 = (s32[1,2,64]{2,1,0:T(2,128)S(1)}, s32[1,2,64]{2,1,0:T(2,128)}, u32[]{:S(2)}) copy-start(s32[1,2,64]{2,1,0:T(2,128)} %param.12) | copy-start | bytes 1540
  140.6 13.4 %copy-start.3 = (f32[128,1]{1,0:T(8,128)S(1)}, f32[128,1]{1,0:T(8,128)}, u32[]{:S(2)}) copy-start(f32[128,1]{1,0:T(8,128)} %get-tuple-element.14) | copy-start | bytes 1540
  140.6 14.2 %copy-start.2 = (bf16[8,48,1280]{2,1,0:T(8,128)(2,1)S(1)}, bf16[8,48,1280]{2,1,0:T(8,128)(2,1)}, u32[]{:S(2)}) copy-start(bf16[8,48,1280]{2,1,0:T(8,128)(2,1)} %get-tuple-element.16) | copy-start | bytes 2949124
  142.8 22.4 %collective-permute-start.1 = (bf16[64,576]{1,0:T(8,128)(2,1)}, bf16[64,576]{1,0:T(8,128)(2,1)}, u32[]{:S(2)}, u32[]{:S(2)}) collective-permute-start(bf16[64,576]{1,0:T(8,128)(2,1)} %bitcast.43), channel_id=1, source_target_pairs={{0,1},{1,0},{2,9},{3,8},{4,17},{5,16},{6,25},{7,24},{8,3},{9,2},{1... | collective-permute-start | bytes 221192 | tf_op jit(solution)/shard_map/ppermute | solution.py:451
  149.0 16.3 %collective-permute-start = (bf16[64,576]{1,0:T(8,128)(2,1)}, bf16[64,576]{1,0:T(8,128)(2,1)}, u32[]{:S(2)}, u32[]{:S(2)}) collective-permute-start(bf16[64,576]{1,0:T(8,128)(2,1)} %bitcast.44), channel_id=1, source_target_pairs={{0,0},{1,1},{2,8},{3,9},{4,16},{5,17},{6,24},{7,25},{8,2},{9,3},{1... | collective-permute-start | bytes 221192 | tf_op jit(solution)/shard_map/ppermute | solution.py:451
  154.9 3.0 %copy-start.1 = (bf16[4,8,16,1152]{3,2,1,0:T(8,128)(2,1)S(1)}, bf16[4,8,16,1152]{3,2,1,0:T(8,128)(2,1)}, u32[]{:S(2)}) copy-start(bf16[4,8,16,1152]{3,2,1,0:T(8,128)(2,1)} %copy.20) | copy-start | bytes 3538948
  157.9 7.4 %copy-start.6 = (s32[2]{0:T(128)S(1)}, s32[2]{0:T(128)}, u32[]{:S(2)}) copy-start(s32[2]{0:T(128)} %fusion.19) | copy-start | bytes 28
